TPU v7x, 32 devices: a whole 2x2x4 slice. The times are simulated.
32 devices in a mesh: section: 2 (over core), fsdp: 16 (over z, y, x).
Axes of the slice: x: 2, y: 2, z: 4, core: 2. Of those that a mesh axis runs over, the one named last changes fastest.
Arguments:
- inputs: bfloat16 [2, 2048, 1600], P(None, 'fsdp'), may hold values from -6 to 6
- cotangent: bfloat16 [2, 2048, 1600], P(None, 'fsdp'), may hold values from -6 to 6
- segments: int32 [2, 2048], P(None, 'fsdp'), may hold values from 0 to 5, as said below
- ln1_gain: bfloat16 [2, 1600], P('section', 'fsdp'), may hold values from 0.5 to 1.5
- ln1_bias: bfloat16 [2, 1600], P('section', 'fsdp'), may hold values from -1.25 to 1.25
- w_qkv: bfloat16 [2, 1600, 4800], P('section', 'fsdp'), may hold values from -0.15625 to 0.15625
- b_qv: bfloat16 [2, 3200], P('section', 'fsdp'), may hold values from -1.25 to 1.25
- w_out: bfloat16 [2, 1600, 1600], P('section', 'fsdp'), may hold values from -1.75 to 1.75
- b_out: bfloat16 [2, 1600], P('section', 'fsdp'), may hold values from -1.25 to 1.25
- ln2_gain: bfloat16 [2, 1600], P('section', 'fsdp'), may hold values from 0.5 to 1.5
- ln2_bias: bfloat16 [2, 1600], P('section', 'fsdp'), may hold values from -1.25 to 1.25
- w_fc: bfloat16 [2, 1600, 6400], P('section', 'fsdp'), may hold values from -0.15625 to 0.15625
- b_fc: bfloat16 [2, 6400], P('section', 'fsdp'), may hold values from -1.25 to 1.25
- w_proj: bfloat16 [2, 1600, 6400], P('section', 'fsdp'), may hold values from -0.078125 to 0.078125
- b_proj: bfloat16 [2, 1600], P('section', 'fsdp'), may hold values from -1.25 to 1.25
Outputs:
- activations: bfloat16 [2, 2, 2048, 1600], P('section', None, 'fsdp')
- input_grad: bfloat16 [2, 2, 2048, 1600], P('section', None, 'fsdp')
- grad_ln1_gain: float32 [2, 1600], P('section', 'fsdp')
- grad_ln1_bias: float32 [2, 1600], P('section', 'fsdp')
- grad_w_qkv: float32 [2, 1600, 4800], P('section', 'fsdp')
- grad_b_qv: float32 [2, 3200], P('section', 'fsdp')
- grad_w_out: float32 [2, 1600, 1600], P('section', 'fsdp')
- grad_b_out: float32 [2, 1600], P('section', 'fsdp')
- grad_ln2_gain: float32 [2, 1600], P('section', 'fsdp')
- grad_ln2_bias: float32 [2, 1600], P('section', 'fsdp')
- grad_w_fc: float32 [2, 1600, 6400], P('section', 'fsdp')
- grad_b_fc: float32 [2, 6400], P('section', 'fsdp')
- grad_w_proj: float32 [2, 1600, 6400], P('section', 'fsdp')
- grad_b_proj: float32 [2, 1600], P('section', 'fsdp')
Inputs may be any that keep to these rules, and one draw needn't show every extreme that they name: `segments`: in each micro-batch, pack k (tokens k * 1024 to (k + 1) * 1024 - 1) holds three documents numbered 3 k, 3 k + 1, 3 k + 2 in order; the middle one has exactly 800 tokens, the first and the last 60 or more; the first has fewer than 128 tokens and the last at most 128.
All inputs are finite; a program needn't handle non-finite values.
Results may differ from a plain program's by a relative error of at most 0.019.
Values may be sent and summed in bfloat16 or wider, within the bound.
No kernel may reach another device: no remote copies, remote signals or barrier semaphores. Data moves between devices by JAX's collectives and lax.ppermute only.
A program may use at most 576 MiB of HBM per device.

v0:
```python
import math

import jax
import jax.numpy as jnp
from jax import lax
from jax.sharding import PartitionSpec as P

HEADS = 25
HEAD_DIM = 64
SEQ_LEN = 1024


def shifted(value, axis, steps):
    count = lax.axis_size(axis)
    first, last = (max(0, -steps), min(count, count - steps))
    return lax.ppermute(value, axis, [(source, source + steps) for source in range(first, last)])


def norm_rows(values, gain_vec, bias_vec):
    row_mean = jnp.mean(values, axis=-1, keepdims=True)
    centered = values - row_mean
    variance = jnp.mean(centered * centered, axis=-1, keepdims=True)
    return centered * lax.rsqrt(variance + 1e-05) * gain_vec + bias_vec


def gelu_tanh(values):
    return jax.nn.gelu(values, approximate=True)


def inner_rows(left, right):
    return lax.dot_general(
        left, right, (((0,), (0,)), ((), ())), preferred_element_type=jnp.float32
    )


def outer_cols(left, right):
    return lax.dot_general(
        left, right, (((1,), (1,)), ((), ())), preferred_element_type=jnp.float32
    )


def unpack(gathered):
    return tuple((member[0] for member in gathered))


def matrix_terms(factors):
    normed, grad_packed, context, grad_attn, normed_two, grad_pre, grad_out_low, activated = factors
    return jnp.concatenate(
        [
            inner_rows(normed, grad_packed),
            inner_rows(context, grad_attn),
            inner_rows(normed_two, grad_pre),
            inner_rows(grad_out_low, activated),
        ],
        axis=1,
    )


def on_device(
    inputs,
    cotangent,
    segments,
    ln1_gain,
    ln1_bias,
    w_qkv,
    b_qv,
    w_out,
    b_out,
    ln2_gain,
    ln2_bias,
    w_fc,
    b_fc,
    w_proj,
    b_proj,
):
    section_index = lax.axis_index("section")
    section_count = lax.axis_size("section")
    fsdp_rank = lax.axis_index("fsdp")
    micro_count, local_rows, model_width = inputs.shape
    seq_devices = max(1, SEQ_LEN // local_rows)
    reach_count = seq_devices - 1
    window_rows = seq_devices * local_rows
    head_count = HEADS
    head_size = HEAD_DIM
    score_scale = 1.0 / math.sqrt(head_size)
    hidden_width = w_fc.shape[2]
    query_index = reach_count * local_rows + jnp.arange(local_rows, dtype=jnp.int32)
    key_index = jnp.arange(window_rows, dtype=jnp.int32)
    causal = key_index[None, :] <= query_index[:, None]
    segment_all = lax.all_gather(segments, "fsdp", axis=1, tiled=True)
    padded_segments = jnp.concatenate(
        [jnp.full((micro_count, reach_count * local_rows), -1, jnp.int32), segment_all], axis=1
    )
    window_segments = lax.dynamic_slice_in_dim(
        padded_segments, fsdp_rank * local_rows, window_rows, 1
    )

    def fetch_weights():
        return unpack(
            (
                lax.all_gather(ln1_gain, "fsdp", axis=1, tiled=True),
                lax.all_gather(ln1_bias, "fsdp", axis=1, tiled=True),
                lax.all_gather(w_qkv, "fsdp", axis=1, tiled=True),
                lax.all_gather(b_qv, "fsdp", axis=1, tiled=True),
                lax.all_gather(w_out, "fsdp", axis=1, tiled=True),
                lax.all_gather(b_out, "fsdp", axis=1, tiled=True),
                lax.all_gather(ln2_gain, "fsdp", axis=1, tiled=True),
                lax.all_gather(ln2_bias, "fsdp", axis=1, tiled=True),
                lax.all_gather(w_fc, "fsdp", axis=1, tiled=True),
                lax.all_gather(b_fc, "fsdp", axis=1, tiled=True),
                lax.all_gather(w_proj, "fsdp", axis=1, tiled=True),
                lax.all_gather(b_proj, "fsdp", axis=1, tiled=True),
            )
        )

    def forward(rows_in, weights_full, key_segments, own_segments):
        (
            gain_one,
            bias_one,
            qkv_weight,
            qv_bias,
            out_weight,
            out_bias,
            gain_two,
            bias_two,
            fc_weight,
            fc_bias,
            proj_weight,
            proj_bias,
        ) = weights_full
        normed_float, norm_back_one = jax.vjp(
            norm_rows, rows_in, gain_one.astype(jnp.float32), bias_one.astype(jnp.float32)
        )
        normed = normed_float.astype(jnp.bfloat16)
        qkv_bias = jnp.concatenate(
            [
                qv_bias[:model_width].astype(jnp.float32),
                jnp.zeros((model_width,), jnp.float32),
                qv_bias[model_width:].astype(jnp.float32),
            ]
        )
        packed = (
            jnp.dot(normed, qkv_weight, preferred_element_type=jnp.float32) + qkv_bias
        ).astype(jnp.bfloat16)
        queries = packed[:, :model_width]
        own_pairs = packed[:, model_width:]
        earlier = []
        for distance in range(reach_count, 0, -1):
            earlier.append(shifted(own_pairs, "fsdp", distance))
        window_pairs = jnp.concatenate(earlier + [own_pairs], axis=0)
        query_heads = queries.reshape(local_rows, head_count, head_size)
        key_heads = window_pairs[:, :model_width].reshape(window_rows, head_count, head_size)
        value_heads = window_pairs[:, model_width:].reshape(window_rows, head_count, head_size)
        allowed = (own_segments[:, None] == key_segments[None, :]) & causal
        scores = (
            jnp.einsum("qhd,khd->hqk", query_heads, key_heads, preferred_element_type=jnp.float32)
            * score_scale
        )
        scores = jnp.where(allowed[None], scores, -1e30)
        row_max = jnp.max(scores, axis=-1, keepdims=True)
        exponent = jnp.exp(scores - row_max)
        attn_probs = exponent / jnp.sum(exponent, axis=-1, keepdims=True)
        probs_low = attn_probs.astype(jnp.bfloat16)
        context = (
            jnp.einsum("hqk,khd->qhd", probs_low, value_heads, preferred_element_type=jnp.float32)
            .reshape(local_rows, model_width)
            .astype(jnp.bfloat16)
        )
        middle = (
            rows_in
            + jnp.dot(context, out_weight, preferred_element_type=jnp.float32)
            + out_bias.astype(jnp.float32)
        )
        normed_two_float, norm_back_two = jax.vjp(
            norm_rows, middle, gain_two.astype(jnp.float32), bias_two.astype(jnp.float32)
        )
        normed_two = normed_two_float.astype(jnp.bfloat16)
        pre_act = jnp.dot(
            normed_two, fc_weight, preferred_element_type=jnp.float32
        ) + fc_bias.astype(jnp.float32)
        activated_float, gelu_back = jax.vjp(gelu_tanh, pre_act)
        activated = activated_float.astype(jnp.bfloat16)
        result = middle + outer_cols(activated, proj_weight) + proj_bias.astype(jnp.float32)
        kept_state = (
            norm_back_one,
            normed,
            query_heads,
            key_heads,
            value_heads,
            attn_probs,
            probs_low,
            context,
            norm_back_two,
            normed_two,
            gelu_back,
            activated,
        )
        return (result, kept_state)

    tick_total = micro_count + section_count - 1
    last_section = section_count - 1
    kept_inputs = jnp.zeros_like(inputs)
    section_outputs = jnp.zeros_like(inputs)
    received = jnp.zeros((local_rows, model_width), jnp.bfloat16)
    forward_weights = fetch_weights()
    for step_index in range(tick_total):
        micro_slot = step_index - section_index
        is_valid = (micro_slot >= 0) & (micro_slot < micro_count)
        slot_index = jnp.clip(micro_slot, 0, micro_count - 1)
        fresh_rows = inputs[min(step_index, micro_count - 1)]
        rows_in = jnp.where(section_index == 0, fresh_rows, received)
        result, kept_state = forward(
            rows_in.astype(jnp.float32),
            forward_weights,
            window_segments[slot_index],
            segments[slot_index],
        )
        result_low = result.astype(jnp.bfloat16)
        kept_inputs = jnp.where(is_valid, kept_inputs.at[slot_index].set(rows_in), kept_inputs)
        section_outputs = jnp.where(
            is_valid, section_outputs.at[slot_index].set(result_low), section_outputs
        )
        if step_index + 1 < tick_total:
            received = shifted(result_low, "section", 1)
    saved_factors = []
    vector_running = (
        jnp.zeros((model_width,), jnp.float32),
        jnp.zeros((model_width,), jnp.float32),
        jnp.zeros((2 * model_width,), jnp.float32),
        jnp.zeros((model_width,), jnp.float32),
        jnp.zeros((model_width,), jnp.float32),
        jnp.zeros((model_width,), jnp.float32),
        jnp.zeros((hidden_width,), jnp.float32),
        jnp.zeros((model_width,), jnp.float32),
    )
    input_grads = jnp.zeros_like(inputs)
    received = jnp.zeros((local_rows, model_width), jnp.bfloat16)
    backward_weights = fetch_weights()
    for step_index in range(tick_total):
        micro_slot = step_index - (last_section - section_index)
        is_valid = (micro_slot >= 0) & (micro_slot < micro_count)
        slot_index = jnp.clip(micro_slot, 0, micro_count - 1)
        fresh_grad = cotangent[min(step_index, micro_count - 1)]
        upstream = jnp.where(
            is_valid & (section_index == last_section), fresh_grad, received
        ).astype(jnp.float32)
        backward_result, backward_kept_state = forward(
            kept_inputs[slot_index].astype(jnp.float32),
            backward_weights,
            window_segments[slot_index],
            segments[slot_index],
        )
        (
            backward_norm_back_one,
            backward_normed,
            backward_query_heads,
            backward_key_heads,
            backward_value_heads,
            backward_attn_probs,
            backward_probs_low,
            backward_context,
            backward_norm_back_two,
            backward_normed_two,
            backward_gelu_back,
            backward_activated,
        ) = backward_kept_state
        backward_qkv_weight = backward_weights[2]
        backward_out_weight = backward_weights[4]
        backward_fc_weight = backward_weights[8]
        backward_proj_weight = backward_weights[10]
        grad_out_low = upstream.astype(jnp.bfloat16)
        grad_act = jnp.dot(grad_out_low, backward_proj_weight, preferred_element_type=jnp.float32)
        grad_pre = backward_gelu_back(grad_act)[0].astype(jnp.bfloat16)
        grad_norm_two = outer_cols(grad_pre, backward_fc_weight)
        grad_middle_norm, grad_gain_two, grad_bias_two = backward_norm_back_two(grad_norm_two)
        grad_middle = upstream + grad_middle_norm
        grad_attn = grad_middle.astype(jnp.bfloat16)
        grad_context = outer_cols(grad_attn, backward_out_weight).astype(jnp.bfloat16)
        context_heads = grad_context.reshape(local_rows, head_count, head_size)
        grad_values = jnp.einsum(
            "hqk,qhd->khd", backward_probs_low, context_heads, preferred_element_type=jnp.float32
        )
        grad_probs = jnp.einsum(
            "qhd,khd->hqk", context_heads, backward_value_heads, preferred_element_type=jnp.float32
        )
        grad_scores = (
            backward_attn_probs
            * (grad_probs - jnp.sum(backward_attn_probs * grad_probs, axis=-1, keepdims=True))
        ).astype(jnp.bfloat16)
        grad_queries = (
            jnp.einsum(
                "hqk,khd->qhd", grad_scores, backward_key_heads, preferred_element_type=jnp.float32
            )
            * score_scale
        )
        grad_keys = (
            jnp.einsum(
                "hqk,qhd->khd",
                grad_scores,
                backward_query_heads,
                preferred_element_type=jnp.float32,
            )
            * score_scale
        )
        grad_pairs = jnp.concatenate(
            [
                grad_keys.reshape(window_rows, model_width),
                grad_values.reshape(window_rows, model_width),
            ],
            axis=1,
        )
        own_grad = grad_pairs[reach_count * local_rows :]
        for backward_distance in range(1, reach_count + 1):
            first_row = (reach_count - backward_distance) * local_rows
            own_grad = own_grad + shifted(
                grad_pairs[first_row : first_row + local_rows].astype(jnp.bfloat16),
                "fsdp",
                -backward_distance,
            ).astype(jnp.float32)
        grad_packed = jnp.concatenate(
            [grad_queries.reshape(local_rows, model_width), own_grad], axis=1
        ).astype(jnp.bfloat16)
        grad_normed = outer_cols(grad_packed, backward_qkv_weight)
        grad_rows_norm, grad_gain_one, grad_bias_one = backward_norm_back_one(grad_normed)
        grad_rows = grad_middle + grad_rows_norm
        factors = (
            backward_normed,
            grad_packed,
            backward_context,
            grad_attn,
            backward_normed_two,
            grad_pre,
            grad_out_low,
            backward_activated,
        )
        packed_float = grad_packed.astype(jnp.float32)
        vector_part = (
            grad_gain_one,
            grad_bias_one,
            jnp.concatenate(
                [
                    jnp.sum(packed_float[:, :model_width], axis=0),
                    jnp.sum(packed_float[:, 2 * model_width :], axis=0),
                ]
            ),
            jnp.sum(grad_attn.astype(jnp.float32), axis=0),
            grad_gain_two,
            grad_bias_two,
            jnp.sum(grad_pre.astype(jnp.float32), axis=0),
            jnp.sum(grad_out_low.astype(jnp.float32), axis=0),
        )
        grad_rows, factors, vector_part = (grad_rows, factors, vector_part)
        saved_factors.append(factors)
        vector_running = tuple(
            (running + addend for running, addend in zip(vector_running, vector_part))
        )
        grad_low = grad_rows.astype(jnp.bfloat16)
        input_grads = jnp.where(is_valid, input_grads.at[slot_index].set(grad_low), input_grads)
        if step_index + 1 < tick_total:
            received = shifted(grad_low, "section", -1)
    joined = tuple(
        (jnp.concatenate([kept[member] for kept in saved_factors], axis=0) for member in range(8))
    )
    matrix_running = lax.psum_scatter(matrix_terms(joined), "fsdp", scatter_dimension=0, tiled=True)
    vector_own = (
        lax.psum_scatter(vector_running[0], "fsdp", scatter_dimension=0, tiled=True),
        lax.psum_scatter(vector_running[1], "fsdp", scatter_dimension=0, tiled=True),
        lax.psum_scatter(vector_running[2], "fsdp", scatter_dimension=0, tiled=True),
        lax.psum_scatter(vector_running[3], "fsdp", scatter_dimension=0, tiled=True),
        lax.psum_scatter(vector_running[4], "fsdp", scatter_dimension=0, tiled=True),
        lax.psum_scatter(vector_running[5], "fsdp", scatter_dimension=0, tiled=True),
        lax.psum_scatter(vector_running[6], "fsdp", scatter_dimension=0, tiled=True),
        lax.psum_scatter(vector_running[7], "fsdp", scatter_dimension=0, tiled=True),
    )
    grad_w_qkv = matrix_running[:, : 3 * model_width]
    grad_w_out = matrix_running[:, 3 * model_width : 4 * model_width]
    grad_w_fc = matrix_running[:, 4 * model_width : 4 * model_width + hidden_width]
    grad_w_proj = matrix_running[:, 4 * model_width + hidden_width :]
    return (
        section_outputs[None],
        input_grads[None],
        vector_own[0][None],
        vector_own[1][None],
        grad_w_qkv[None],
        vector_own[2][None],
        grad_w_out[None],
        vector_own[3][None],
        vector_own[4][None],
        vector_own[5][None],
        grad_w_fc[None],
        vector_own[6][None],
        grad_w_proj[None],
        vector_own[7][None],
    )


def solution(mesh):
    in_specs = (
        P(None, "fsdp", None),
        P(None, "fsdp", None),
        P(None, "fsdp"),
        P("section", "fsdp"),
        P("section", "fsdp"),
        P("section", "fsdp", None),
        P("section", "fsdp"),
        P("section", "fsdp", None),
        P("section", "fsdp"),
        P("section", "fsdp"),
        P("section", "fsdp"),
        P("section", "fsdp", None),
        P("section", "fsdp"),
        P("section", "fsdp", None),
        P("section", "fsdp"),
    )
    out_specs = (
        P("section", None, "fsdp", None),
        P("section", None, "fsdp", None),
        P("section", "fsdp"),
        P("section", "fsdp"),
        P("section", "fsdp", None),
        P("section", "fsdp"),
        P("section", "fsdp", None),
        P("section", "fsdp"),
        P("section", "fsdp"),
        P("section", "fsdp"),
        P("section", "fsdp", None),
        P("section", "fsdp"),
        P("section", "fsdp", None),
        P("section", "fsdp"),
    )
    return jax.shard_map(
        on_device, mesh=mesh, in_specs=in_specs, out_specs=out_specs, check_vma=False
    )
```

profile of v0, /device:TPU:0, one launch (start us, length us, event | category | flops | bytes accessed | tf_op | source)
XLA Modules:
  0.0 6670.2 jit_solution(5046499611632832018)
XLA Ops:
  26.1 81.3 %all-reduce.19 = (bf16[3200]{0:T(1024)(128)(2,1)S(1)}, bf16[1600]{0:T(1024)(128)(2,1)S(1)}, bf16[1600]{0:T(1024)(128)(2,1)S(1)}, bf16[1600]{0:T(1024)(128)(2,1)S...) all-reduce(bf16[3200]{0:T(1024)(128)(2,1)S(1)} %dynamic-update-slic, ...), channel_id=1, replica_groups=mesh['section'=2,'fsdp'=16] {'fsdp'}, use_global_device_ids=true, to_apply=%add.3 | all-reduce | flops 19200 | bytes 76800
  108.2 235.4 %all-gather.5.cloned.1.call-done = bf16[1,1600,4800]{2,0,1:T(2,128)(2,1)} async-done(((bf16[1,100,4800]{2,0,1:T(2,128)(2,1)}), bf16[1,1600,4800]{2,0,1:T(2,128)(2,1)}) %all-gather.5.cloned.1.call-update) | async-done | bytes 15360016 | tf_op jit(solution)/shard_map/all_gather | solution.py:103
  379.8 67.9 %all_gather.54 = s32[2,2048]{1,0:T(2,128)S(1)} all-gather(s32[2,128]{1,0:T(2,128)S(1)} %copy-done.122), channel_id=1, replica_groups=mesh['section'=2,'fsdp'=16] {'fsdp'}, dimensions={1}, use_global_device_ids=true | all-gather | bytes 17408 | tf_op jit(solution)/shard_map/all_gather | solution.py:90
  475.6 48.3 all-gather.7.cloned.1.call-done
  597.9 34.3 collective-permute-done.3
  659.7 397.4 %all-gather.9.cloned.1.call-done = bf16[1,1600,6400]{2,0,1:T(2,128)(2,1)} async-done(((bf16[1,100,6400]{2,0,1:T(2,128)(2,1)}), bf16[1,1600,6400]{2,0,1:T(2,128)(2,1)}) %all-gather.9.cloned.1.call-update) | async-done | bytes 20480016 | tf_op jit(solution)/shard_map/all_gather | solution.py:109
  1090.9 388.4 %all-gather.11.cloned.1.call-done = bf16[1,1600,6400]{2,0,1:T(2,128)(2,1)} async-done(((bf16[1,100,6400]{2,0,1:T(2,128)(2,1)}), bf16[1,1600,6400]{2,0,1:T(2,128)(2,1)}) %all-gather.11.cloned.1.call-update) | async-done | bytes 20480016 | tf_op jit(solution)/shard_map/all_gather | solution.py:111
  1677.5 119.7 %collective-permute-start.23 = (bf16[128,3200]{0,1:T(8,128)(2,1)}, bf16[128,3200]{0,1:T(8,128)(2,1)}, u32[]{:S(2)}, u32[]{:S(2)}) collective-permute-start(bf16[128,3200]{0,1:T(8,128)(2,1)} %slice.476), channel_id=1, source_target_pairs={{0,7},{1,8},{2,9},{3,10},{4,11},{5,12},{6,13},{7,14},{8,15},{16,23... | collective-permute-start | bytes 2457608 | tf_op jit(solution)/shard_map/ppermute | solution.py:16
  1988.8 56.0 collective-permute-done.30
  2046.1 29.2 collective-permute-done.36
  2128.2 59.3 collective-permute-start.38
  2193.0 81.5 %collective-permute-start.39 = (bf16[128,3200]{0,1:T(8,128)(2,1)}, bf16[128,3200]{0,1:T(8,128)(2,1)S(1)}, u32[]{:S(2)}, u32[]{:S(2)}) collective-permute-start(bf16[128,3200]{0,1:T(8,128)(2,1)} %slice.489), channel_id=1, source_target_pairs={{0,6},{1,7},{2,8},{3,9},{4,10},{5,11},{6,12},{7,13},{8,14},{9,15},... | collective-permute-start | bytes 2457608 | tf_op jit(solution)/shard_map/ppermute | solution.py:16
  2456.1 63.9 collective-permute-done.45
  2612.0 34.5 collective-permute-start.59
  2663.8 55.5 collective-permute-start.57
  2739.3 34.3 collective-permute-start.55
  2972.1 60.6 collective-permute-done.60
  3034.0 45.2 collective-permute-done.66
  3143.5 141.9 %concatenate.144 = f32[1600,19200]{1,0:T(8,128)} concatenate(f32[1600,4800]{1,0:T(8,128)} %fusion.168, f32[1600,1600]{1,0:T(8,128)} %fusion.406, f32[1600,6400]{1,0:T(8,128)} %fusion.156, f32[1600,6400]{1,0:T(8,128)} %fusion.162), dimensions={1} | concatenate | bytes 245760000 | tf_op jit(solution)/shard_map/concatenate | solution.py:48
  3300.1 61.7 collective-permute-start.16
  3361.9 59.1 collective-permute-start.17
  3431.8 44.3 collective-permute-start.18
  3480.6 31.8 collective-permute-done.18
  3606.4 3036.4 %all-reduce.23.cloned.1.call-done = f32[1600,19200]{1,0:T(8,128)} async-done(((f32[1600,19200]{1,0:T(8,128)}), f32[1600,19200]{1,0:T(8,128)}) %all-reduce.23.cloned.1.call-update) | async-done | bytes 122880016
  (855 shorter events, 1379.9 us)
Async XLA Ops:
  7.2 336.3 %all-gather.5.cloned.1.call-start = ((), (), s32[]{:S(2)}) async-start(), calls=%async_computation | async-start | bytes 33075200 | tf_op jit(solution)/shard_map/all_gather | solution.py:103
  11.4 512.5 %all-gather.7.cloned.1.call-start = ((), (), s32[]{:S(2)}) async-start(), calls=%async_computation.1 | async-start | bytes 11315200 | tf_op jit(solution)/shard_map/all_gather | solution.py:105
  12.8 1044.4 %all-gather.9.cloned.1.call-start = ((), (), s32[]{:S(2)}) async-start(), calls=%async_computation.2 | async-start | bytes 43520000 | tf_op jit(solution)/shard_map/all_gather | solution.py:109
  16.4 1462.9 %all-gather.11.cloned.1.call-start = ((), (), s32[]{:S(2)}) async-start(), calls=%async_computation.3 | async-start | bytes 43520000 | tf_op jit(solution)/shard_map/all_gather | solution.py:111
  21.4 3574.7 %all-reduce.25.cloned.1.call-start = ((), (), s32[]{:S(2)}) async-start(), calls=%async_computation.5 | async-start | bytes 188416
  375.9 184.3 %collective-permute-start = (bf16[128,3200]{0,1:T(8,128)(2,1)S(1)}, bf16[128,3200]{0,1:T(8,128)(2,1)}, u32[]{:S(2)}, u32[]{:S(2)}) collective-permute-start(bf16[128,3200]{0,1:T(8,128)(2,1)S(1)} %slice.464), channel_id=1, source_target_pairs={{0,7},{1,8},{2,9},{3,10},{4,11},{5,12},{6,13},{7,14},{8,15},{16,23... | collective-permute-start | bytes 2457608 | tf_op jit(solution)/shard_map/ppermute | solution.py:16
  448.6 114.3 %collective-permute-start.1 = (bf16[128,3200]{0,1:T(8,128)(2,1)S(1)}, bf16[128,3200]{0,1:T(8,128)(2,1)}, u32[]{:S(2)}, u32[]{:S(2)}) collective-permute-start(bf16[128,3200]{0,1:T(8,128)(2,1)S(1)} %slice.464), channel_id=1, source_target_pairs={{0,6},{1,7},{2,8},{3,9},{4,10},{5,11},{6,12},{7,13},{8,14},{9,15},... | collective-permute-start | bytes 2457608 | tf_op jit(solution)/shard_map/ppermute | solution.py:16
  1677.5 149.2 %collective-permute-start.23 = (bf16[128,3200]{0,1:T(8,128)(2,1)}, bf16[128,3200]{0,1:T(8,128)(2,1)}, u32[]{:S(2)}, u32[]{:S(2)}) collective-permute-start(bf16[128,3200]{0,1:T(8,128)(2,1)} %slice.476), channel_id=1, source_target_pairs={{0,7},{1,8},{2,9},{3,10},{4,11},{5,12},{6,13},{7,14},{8,15},{16,23... | collective-permute-start | bytes 2457608 | tf_op jit(solution)/shard_map/ppermute | solution.py:16
  2128.2 157.6 %collective-permute-start.38 = (bf16[128,3200]{0,1:T(8,128)(2,1)}, bf16[128,3200]{0,1:T(8,128)(2,1)}, u32[]{:S(2)}, u32[]{:S(2)}) collective-permute-start(bf16[128,3200]{0,1:T(8,128)(2,1)} %slice.489), channel_id=1, source_target_pairs={{0,7},{1,8},{2,9},{3,10},{4,11},{5,12},{6,13},{7,14},{8,15},{16,23... | collective-permute-start | bytes 2457608 | tf_op jit(solution)/shard_map/ppermute | solution.py:16
  2193.0 114.0 %collective-permute-start.39 = (bf16[128,3200]{0,1:T(8,128)(2,1)}, bf16[128,3200]{0,1:T(8,128)(2,1)S(1)}, u32[]{:S(2)}, u32[]{:S(2)}) collective-permute-start(bf16[128,3200]{0,1:T(8,128)(2,1)} %slice.489), channel_id=1, source_target_pairs={{0,6},{1,7},{2,8},{3,9},{4,10},{5,11},{6,12},{7,13},{8,14},{9,15},... | collective-permute-start | bytes 2457608 | tf_op jit(solution)/shard_map/ppermute | solution.py:16
  2452.2 116.3 %collective-permute-start.50 = (bf16[128,3200]{0,1:T(8,128)(2,1)}, bf16[128,3200]{0,1:T(8,128)(2,1)S(1)}, u32[]{:S(2)}, u32[]{:S(2)}) collective-permute-start(bf16[128,3200]{0,1:T(8,128)(2,1)} %get-tuple-element.259), channel_id=1, source_target_pairs={{6,0},{7,1},{8,2},{9,3},{10,4},{11,5},{12,6},{13,7},{14,8},{15,9},... | collective-permute-start | bytes 2457608 | tf_op jit(solution)/shard_map/ppermute | solution.py:16
  2453.5 115.1 %collective-permute-start.49 = (bf16[128,3200]{0,1:T(8,128)(2,1)}, bf16[128,3200]{0,1:T(8,128)(2,1)S(1)}, u32[]{:S(2)}, u32[]{:S(2)}) collective-permute-start(bf16[128,3200]{0,1:T(8,128)(2,1)} %get-tuple-element.260), channel_id=1, source_target_pairs={{5,0},{6,1},{7,2},{8,3},{9,4},{10,5},{11,6},{12,7},{13,8},{14,9},{... | collective-permute-start | bytes 2457608 | tf_op jit(solution)/shard_map/ppermute | solution.py:16
  2612.0 194.6 %collective-permute-start.59 = (bf16[128,3200]{0,1:T(8,128)(2,1)S(1)}, bf16[128,3200]{0,1:T(8,128)(2,1)S(1)}, u32[]{:S(2)}, u32[]{:S(2)}) collective-permute-start(bf16[128,3200]{0,1:T(8,128)(2,1)S(1)} %slice.502), channel_id=1, source_target_pairs={{0,1},{1,2},{2,3},{3,4},{4,5},{5,6},{6,7},{7,8},{8,9},{9,10},{10,1... | collective-permute-start | bytes 2457608 | tf_op jit(solution)/shard_map/ppermute | solution.py:16
  2646.6 159.7 %collective-permute-start.58 = (bf16[128,3200]{0,1:T(8,128)(2,1)S(1)}, bf16[128,3200]{0,1:T(8,128)(2,1)S(1)}, u32[]{:S(2)}, u32[]{:S(2)}) collective-permute-start(bf16[128,3200]{0,1:T(8,128)(2,1)S(1)} %slice.502), channel_id=1, source_target_pairs={{0,2},{1,3},{2,4},{3,5},{4,6},{5,7},{6,8},{7,9},{8,10},{9,11},{10,... | collective-permute-start | bytes 2457608 | tf_op jit(solution)/shard_map/ppermute | solution.py:16
  2663.8 142.2 %collective-permute-start.57 = (bf16[128,3200]{0,1:T(8,128)(2,1)S(1)}, bf16[128,3200]{0,1:T(8,128)(2,1)S(1)}, u32[]{:S(2)}, u32[]{:S(2)}) collective-permute-start(bf16[128,3200]{0,1:T(8,128)(2,1)S(1)} %slice.502), channel_id=1, source_target_pairs={{0,3},{1,4},{2,5},{3,6},{4,7},{5,8},{6,9},{7,10},{8,11},{9,12},{10... | collective-permute-start | bytes 2457608 | tf_op jit(solution)/shard_map/ppermute | solution.py:16
  2935.9 143.2 %collective-permute-start.66 = (bf16[128,3200]{0,1:T(8,128)(2,1)}, bf16[128,3200]{0,1:T(8,128)(2,1)}, u32[]{:S(2)}, u32[]{:S(2)}) collective-permute-start(bf16[128,3200]{0,1:T(8,128)(2,1)} %get-tuple-element.249), channel_id=1, source_target_pairs={{7,0},{8,1},{9,2},{10,3},{11,4},{12,5},{13,6},{14,7},{15,8},{23,16... | collective-permute-start | bytes 2457608 | tf_op jit(solution)/shard_map/ppermute | solution.py:16
  2937.2 149.6 %collective-permute-start.65 = (bf16[128,3200]{0,1:T(8,128)(2,1)}, bf16[128,3200]{0,1:T(8,128)(2,1)}, u32[]{:S(2)}, u32[]{:S(2)}) collective-permute-start(bf16[128,3200]{0,1:T(8,128)(2,1)} %get-tuple-element.250), channel_id=1, source_target_pairs={{6,0},{7,1},{8,2},{9,3},{10,4},{11,5},{12,6},{13,7},{14,8},{15,9},... | collective-permute-start | bytes 2457608 | tf_op jit(solution)/shard_map/ppermute | solution.py:16
  2938.5 148.3 %collective-permute-start.64 = (bf16[128,3200]{0,1:T(8,128)(2,1)}, bf16[128,3200]{0,1:T(8,128)(2,1)}, u32[]{:S(2)}, u32[]{:S(2)}) collective-permute-start(bf16[128,3200]{0,1:T(8,128)(2,1)} %get-tuple-element.251), channel_id=1, source_target_pairs={{5,0},{6,1},{7,2},{8,3},{9,4},{10,5},{11,6},{12,7},{13,8},{14,9},{... | collective-permute-start | bytes 2457608 | tf_op jit(solution)/shard_map/ppermute | solution.py:16
  2939.8 147.1 %collective-permute-start.63 = (bf16[128,3200]{0,1:T(8,128)(2,1)}, bf16[128,3200]{0,1:T(8,128)(2,1)}, u32[]{:S(2)}, u32[]{:S(2)}) collective-permute-start(bf16[128,3200]{0,1:T(8,128)(2,1)} %get-tuple-element.252), channel_id=1, source_target_pairs={{4,0},{5,1},{6,2},{7,3},{8,4},{9,5},{10,6},{11,7},{12,8},{13,9},{1... | collective-permute-start | bytes 2457608 | tf_op jit(solution)/shard_map/ppermute | solution.py:16
  3127.0 3515.8 %all-reduce.23.cloned.1.call-start = ((), (), s32[]{:S(2)}) async-start(), calls=%async_computation.4 | async-start | bytes 245760000
  3300.1 131.6 %collective-permute-start.16 = (bf16[128,3200]{0,1:T(8,128)(2,1)}, bf16[128,3200]{0,1:T(8,128)(2,1)}, u32[]{:S(2)}, u32[]{:S(2)}) collective-permute-start(bf16[128,3200]{0,1:T(8,128)(2,1)} %slice.472), channel_id=1, source_target_pairs={{0,7},{1,8},{2,9},{3,10},{4,11},{5,12},{6,13},{7,14},{8,15},{16,23... | collective-permute-start | bytes 2457608 | tf_op jit(solution)/shard_map/ppermute | solution.py:16
  3361.9 115.6 %collective-permute-start.17 = (bf16[128,3200]{0,1:T(8,128)(2,1)}, bf16[128,3200]{0,1:T(8,128)(2,1)}, u32[]{:S(2)}, u32[]{:S(2)}) collective-permute-start(bf16[128,3200]{0,1:T(8,128)(2,1)} %slice.472), channel_id=1, source_target_pairs={{0,6},{1,7},{2,8},{3,9},{4,10},{5,11},{6,12},{7,13},{8,14},{9,15},... | collective-permute-start | bytes 2457608 | tf_op jit(solution)/shard_map/ppermute | solution.py:16
  3423.9 116.1 %collective-permute-start.22 = (bf16[128,3200]{0,1:T(8,128)(2,1)}, bf16[128,3200]{0,1:T(8,128)(2,1)S(1)}, u32[]{:S(2)}, u32[]{:S(2)}) collective-permute-start(bf16[128,3200]{0,1:T(8,128)(2,1)} %slice.472), channel_id=1, source_target_pairs={{0,1},{1,2},{2,3},{3,4},{4,5},{5,6},{6,7},{7,8},{8,9},{9,10},{10,1... | collective-permute-start | bytes 2457608 | tf_op jit(solution)/shard_map/ppermute | solution.py:16
  3425.3 114.5 %collective-permute-start.21 = (bf16[128,3200]{0,1:T(8,128)(2,1)}, bf16[128,3200]{0,1:T(8,128)(2,1)S(1)}, u32[]{:S(2)}, u32[]{:S(2)}) collective-permute-start(bf16[128,3200]{0,1:T(8,128)(2,1)} %slice.472), channel_id=1, source_target_pairs={{0,2},{1,3},{2,4},{3,5},{4,6},{5,7},{6,8},{7,9},{8,10},{9,11},{10,... | collective-permute-start | bytes 2457608 | tf_op jit(solution)/shard_map/ppermute | solution.py:16
  (262 other events, 25463.0 us)
Sparse Core Ops, SparseCore 0:
  11.5 332.0 all-gather.4
  346.8 177.0 all-gather.6
  527.2 529.9 all-gather.8
  1060.3 418.9 all-gather.10
  3127.1 216.2 all-reduce.24
  3349.7 3293.0 all-reduce.22
where the time goes:
time: 6680 us; the launch traced here: 6670 us
  waiting for transfers between devices  4760 us (71%)
  starting transfers between devices  770 us (12%)
  matrix products  526 us (8%)
  local copies, waits for them, and re-layouts  337 us (5%)
  blocking collectives  149 us (2%)
  other arithmetic  102 us (2%)
    unnamed x8, waiting for transfers between devices  3040 us
    ppermute x67, starting transfers between devices, shifted(): lax.ppermute(value, axis, [(source, source + steps) for source in range(f...  769 us
    ppermute x67, waiting for transfers between devices, shifted(): lax.ppermute(value, axis, [(source, source + steps) for source in range(f...  658 us
    all_gather x1, waiting for transfers between devices, fetch_weights(): lax.all_gather(w_fc, 'fsdp', axis=1, tiled=True)  397 us
    all_gather x1, waiting for transfers between devices, fetch_weights(): lax.all_gather(w_proj, 'fsdp', axis=1, tiled=True)  388 us
    all_gather x1, waiting for transfers between devices, fetch_weights(): lax.all_gather(w_qkv, 'fsdp', axis=1, tiled=True)  235 us
    unnamed x498, local copies, waits for them, and re-layouts  144 us
    concatenate x1, local copies, waits for them, and re-layouts, matrix_terms(): jnp.concatenate([inner_rows(normed, grad_packed), inner_rows(context, gra...  142 us
  transfers between devices with their start and end apart: 73, of which 39 were waited for; matrix products, arithmetic and copies ran while one was open for 6% of the time, Pallas kernels for 0%

commit v1 on v0

v1 whole, which is shorter than its diff:
```python
import math

import jax
import jax.numpy as jnp
from jax import lax
from jax.experimental import pallas as pl
from jax.experimental.pallas import tpu as pltpu
from jax.sharding import PartitionSpec as P

HEADS = 25
HEAD_DIM = 64
SEQ_LEN = 1024
PACK_DEVS = 8
MAIN = HEADS // PACK_DEVS
SLOTS = 4
SLOT_COLS = SLOTS * HEAD_DIM
BLOCK = 256
BF = jnp.bfloat16
F32 = jnp.float32


def chip_swap(value, mask):
    count = lax.axis_size("fsdp")
    return lax.ppermute(value, "fsdp", [(i, i ^ mask) for i in range(count)])


def core_swap(value):
    return lax.ppermute(value, "section", [(0, 1), (1, 0)])


def ordered(bit, own, other, axis):
    return jnp.where(
        bit == 0,
        jnp.concatenate([own, other], axis=axis),
        jnp.concatenate([other, own], axis=axis),
    )


def take(value, index, size, axis):
    return lax.dynamic_slice_in_dim(value, index * size, size, axis)


def dot(left, right):
    return jnp.dot(left, right, preferred_element_type=F32)


def dot_rows(left, right):
    return lax.dot_general(left, right, (((0,), (0,)), ((), ())), preferred_element_type=F32)


def dot_cols(left, right):
    return lax.dot_general(left, right, (((1,), (1,)), ((), ())), preferred_element_type=F32)


def norm_rows(values, gain_vec, bias_vec):
    row_mean = jnp.mean(values, axis=-1, keepdims=True)
    centered = values - row_mean
    variance = jnp.mean(centered * centered, axis=-1, keepdims=True)
    return centered * lax.rsqrt(variance + 1e-05) * gain_vec + bias_vec


def gelu_tanh(values):
    return jax.nn.gelu(values, approximate=True)


def attend_kernel(q_ref, k_ref, v_ref, srow_ref, scol_ref, ctx_ref, p_ref, bias_ref):
    blocks = q_ref.shape[0] // BLOCK

    @pl.when(pl.program_id(0) == 0)
    def _():
        for i in range(blocks):
            rows = slice(i * BLOCK, (i + 1) * BLOCK)
            wide = (i + 1) * BLOCK
            r = lax.broadcasted_iota(jnp.int32, (BLOCK, wide), 0) + i * BLOCK
            c = lax.broadcasted_iota(jnp.int32, (BLOCK, wide), 1)
            same = scol_ref[rows, :] == srow_ref[:, :wide]
            bias_ref[rows, :wide] = jnp.where(same & (c <= r), 0.0, -1e30)

    for h in range(2):
        lanes = slice(h * HEAD_DIM, (h + 1) * HEAD_DIM)
        for i in range(blocks):
            rows = slice(i * BLOCK, (i + 1) * BLOCK)
            wide = (i + 1) * BLOCK
            q = q_ref[rows, lanes] * jnp.asarray(1.0 / math.sqrt(HEAD_DIM), BF)
            s = dot_cols(q, k_ref[:wide, lanes]) + bias_ref[rows, :wide]
            m = jnp.max(s, axis=-1, keepdims=True)
            e = jnp.exp(s - m)
            p = (e * (1.0 / jnp.sum(e, axis=-1, keepdims=True))).astype(BF)
            p_ref[h, rows, :wide] = p
            ctx_ref[rows, lanes] = dot(p, v_ref[:wide, lanes]).astype(BF)


def attend_back_kernel(q_ref, k_ref, v_ref, p_ref, d_ref, dq_ref, dk_ref, dv_ref, dk_sum, dv_sum):
    blocks = q_ref.shape[0] // BLOCK
    scale = jnp.asarray(1.0 / math.sqrt(HEAD_DIM), BF)
    for h in range(2):
        lanes = slice(h * HEAD_DIM, (h + 1) * HEAD_DIM)
        for i in reversed(range(blocks)):
            rows = slice(i * BLOCK, (i + 1) * BLOCK)
            wide = (i + 1) * BLOCK
            d = d_ref[rows, lanes]
            p_low = p_ref[h, rows, :wide]
            dp = dot_cols(d, v_ref[:wide, lanes])
            p = p_low.astype(F32)
            ds = (p * (dp - jnp.sum(p * dp, axis=-1, keepdims=True))).astype(BF)
            dq_ref[rows, lanes] = dot(ds, k_ref[:wide, lanes] * scale).astype(BF)
            dk = dot_rows(ds, q_ref[rows, lanes] * scale)
            dv = dot_rows(p_low, d)
            if i == blocks - 1:
                dk_sum[...] = dk
                dv_sum[...] = dv
            else:
                dk_sum[:wide, :] += dk
                dv_sum[:wide, :] += dv
        dk_ref[:, lanes] = dk_sum[...].astype(BF)
        dv_ref[:, lanes] = dv_sum[...].astype(BF)


def attend(packed, segs):
    length = packed.shape[0]
    pairs = SLOTS // 2
    lanes = 2 * HEAD_DIM
    return pl.pallas_call(
        attend_kernel,
        grid=(pairs,),
        in_specs=[
            pl.BlockSpec((length, lanes), lambda g: (0, g)),
            pl.BlockSpec((length, lanes), lambda g: (0, pairs + g)),
            pl.BlockSpec((length, lanes), lambda g: (0, 2 * pairs + g)),
            pl.BlockSpec((1, length), lambda g: (0, 0)),
            pl.BlockSpec((length, 1), lambda g: (0, 0)),
        ],
        out_specs=[
            pl.BlockSpec((length, lanes), lambda g: (0, g)),
            pl.BlockSpec((2, length, length), lambda g: (g, 0, 0)),
        ],
        out_shape=[
            jax.ShapeDtypeStruct((length, SLOT_COLS), BF),
            jax.ShapeDtypeStruct((SLOTS, length, length), BF),
        ],
        scratch_shapes=[pltpu.VMEM((length, length), F32)],
        compiler_params=pltpu.CompilerParams(vmem_limit_bytes=48 * 1024 * 1024),
        cost_estimate=pl.CostEstimate(flops=12 * 10**9, bytes_accessed=12 * 10**6, transcendentals=0),
    )(packed, packed, packed, segs.reshape(1, length), segs.reshape(length, 1))


def attend_back(packed, probs, grad):
    length = packed.shape[0]
    pairs = SLOTS // 2
    lanes = 2 * HEAD_DIM
    pair_block = pl.BlockSpec((length, lanes), lambda g: (0, g))
    return pl.pallas_call(
        attend_back_kernel,
        grid=(pairs,),
        in_specs=[
            pair_block,
            pl.BlockSpec((length, lanes), lambda g: (0, pairs + g)),
            pl.BlockSpec((length, lanes), lambda g: (0, 2 * pairs + g)),
            pl.BlockSpec((2, length, length), lambda g: (g, 0, 0)),
            pair_block,
        ],
        out_specs=[pair_block] * 3,
        out_shape=[jax.ShapeDtypeStruct((length, SLOT_COLS), BF)] * 3,
        scratch_shapes=[pltpu.VMEM((length, HEAD_DIM), F32)] * 2,
        compiler_params=pltpu.CompilerParams(vmem_limit_bytes=48 * 1024 * 1024),
        cost_estimate=pl.CostEstimate(flops=24 * 10**9, bytes_accessed=12 * 10**6, transcendentals=0),
    )(packed, packed, packed, probs, grad)


def to_slots(values):
    tokens = values.shape[0]
    split = PACK_DEVS * MAIN * HEAD_DIM
    main = values[:, :split].reshape(tokens, PACK_DEVS, MAIN * HEAD_DIM).transpose(1, 0, 2)
    last = values[None, :, split:]
    none = jnp.zeros((PACK_DEVS - 1,) + last.shape[1:], values.dtype)
    return jnp.concatenate([main, jnp.concatenate([last, none], axis=0)], axis=2)


def from_slots(slots):
    tokens = slots.shape[1]
    main = slots[:, :, : MAIN * HEAD_DIM].transpose(1, 0, 2).reshape(tokens, -1)
    return jnp.concatenate([main, slots[0, :, MAIN * HEAD_DIM :]], axis=1)


def pack_exchange(value):
    count = lax.axis_size("fsdp")
    groups = [list(range(first, first + PACK_DEVS)) for first in range(0, count, PACK_DEVS)]
    return lax.all_to_all(value, "fsdp", 0, 0, axis_index_groups=groups)


def gather_plane(quarter):
    half = quarter.shape[1] // 2
    by_x = chip_swap(quarter, 1)
    by_y = chip_swap(quarter, 2)
    left = chip_swap(by_x[:, :half], 2)
    right = chip_swap(by_y[:, half:], 1)
    return [quarter, by_x, by_y, jnp.concatenate([left, right], axis=1)]


def reduce_plane(parts):
    own, to_x, to_y, across = parts
    half = own.shape[1] // 2
    left = chip_swap(across[:, :half], 2)
    right = chip_swap(across[:, half:], 1)
    to_x = jnp.concatenate(
        [(to_x[:, :half].astype(F32) + left.astype(F32)).astype(BF), to_x[:, half:]], axis=1
    )
    to_y = jnp.concatenate(
        [to_y[:, :half], (to_y[:, half:].astype(F32) + right.astype(F32)).astype(BF)], axis=1
    )
    from_x = chip_swap(to_x, 1)
    from_y = chip_swap(to_y, 2)
    return own.astype(F32) + from_x.astype(F32) + from_y.astype(F32)


def bits_of(count):
    return count.bit_length() - 1


def gather_vector(value):
    index = lax.axis_index("fsdp")
    rows = value[None]
    for bit in range(bits_of(lax.axis_size("fsdp"))):
        rows = ordered((index >> bit) & 1, rows, chip_swap(rows, 1 << bit), 0)
    return rows


def reduce_vector(rows):
    index = lax.axis_index("fsdp")
    for bit in reversed(range(bits_of(lax.axis_size("fsdp")))):
        mine = (index >> bit) & 1
        half = rows.shape[0] // 2
        rows = take(rows, mine, half, 0) + chip_swap(take(rows, 1 - mine, half, 0), 1 << bit)
    return rows[0]


def on_device(
    inputs,
    cotangent,
    segments,
    ln1_gain,
    ln1_bias,
    w_qkv,
    b_qv,
    w_out,
    b_out,
    ln2_gain,
    ln2_bias,
    w_fc,
    b_fc,
    w_proj,
    b_proj,
):
    core = lax.axis_index("section")
    rank = lax.axis_index("fsdp")
    count = lax.axis_size("fsdp")
    bits = bits_of(count)
    tokens, width = inputs.shape[1:]
    shard = w_qkv.shape[1]
    hidden = w_fc.shape[2]
    quarter = width // 4
    high = count // 4
    pair_bit = (rank >> 2) & 1
    plane = rank & 3

    place = jnp.arange(width, dtype=jnp.int32)
    natural = ((place % quarter) // shard * 4 + ((place // quarter) ^ plane)) * shard + place % shard
    order = (jnp.arange(width, dtype=jnp.int32)[:, None] == natural[None, :]).astype(BF)

    def to_own(values):
        return dot(values, order).astype(BF)

    def to_natural(values):
        return dot_cols(values, order).astype(BF)

    def to_own_wide(values):
        top = values.astype(BF)
        return dot(top, order) + dot((values - top.astype(F32)).astype(BF), order)

    vectors = jnp.concatenate(
        [
            ln1_gain[0],
            ln1_bias[0],
            b_out[0],
            ln2_gain[0],
            ln2_bias[0],
            b_proj[0],
            b_qv[0],
            b_fc[0],
            lax.dynamic_index_in_dim(segments, core, 0, False).astype(BF),
        ]
    )
    vector_rows = gather_vector(vectors)
    segment_rows = vector_rows[:, 12 * shard :].astype(jnp.int32)
    pack_segments = take(segment_rows, rank // PACK_DEVS, PACK_DEVS, 0).reshape(-1)
    vector_rows = vector_rows[:, : 12 * shard]
    vector_other = core_swap(vector_rows)
    layer_vectors = []
    for layer in range(2):
        rows = jnp.where(core == layer, vector_rows, vector_other)
        model = jnp.stack([rows[:, i * shard : (i + 1) * shard].reshape(width) for i in range(6)])
        model = dot(model, order)
        qv = rows[:, 6 * shard : 8 * shard].reshape(2 * width).astype(F32)
        fc = rows[:, 8 * shard : 12 * shard].reshape(hidden).astype(F32)
        fc = lax.dynamic_slice_in_dim(fc, core * (hidden // 2) + pair_bit * (hidden // 4), hidden // 4, 0)
        qkv = jnp.concatenate([qv[:width], jnp.zeros((width,), F32), qv[width:]])
        layer_vectors.append((model, qkv, fc))

    def by_core(pieces):
        mine = jnp.concatenate([take(p, core, p.shape[1] // 2, 1) for p in pieces], axis=1)
        yours = jnp.concatenate([take(p, 1 - core, p.shape[1] // 2, 1) for p in pieces], axis=1)
        got = core_swap(yours)
        return [jnp.where(core == layer, mine, got) for layer in range(2)]

    def gather_high(rows, first_bit):
        for bit in range(first_bit, bits):
            rows = ordered((rank >> bit) & 1, rows, chip_swap(rows, 1 << bit), 0)
        return rows

    attn_shards = by_core([w_qkv[0], w_out[0]])
    mlp_shards = by_core([w_fc[0], w_proj[0]])

    def gather_attn(layer):
        rows = gather_high(attn_shards[layer][None], 2).reshape(quarter, -1)
        parts = gather_plane(rows)
        own = jnp.concatenate(parts, axis=0)
        other = jnp.concatenate([core_swap(part) for part in parts], axis=0)
        cut = w_qkv.shape[2] // 2
        return own[:, :cut], other[:, :cut], own[:, cut:], other[:, cut:]

    def gather_mlp(layer):
        both = mlp_shards[layer]
        half = hidden // 2
        small = hidden // 4
        fc_cols, proj_cols = both[:, :half], both[:, half:]
        mine = jnp.concatenate([take(fc_cols, pair_bit, small, 1), take(proj_cols, pair_bit, small, 1)], axis=1)
        yours = jnp.concatenate(
            [take(fc_cols, 1 - pair_bit, small, 1), take(proj_cols, 1 - pair_bit, small, 1)], axis=1
        )
        rows = ordered(pair_bit, mine[None], chip_swap(yours, 4)[None], 0)
        rows = gather_high(rows, 3).reshape(quarter, -1)
        full = jnp.concatenate(gather_plane(rows), axis=0)
        return full[:, :small], full[:, small:]

    attn_weights = [None, None]
    mlp_weights = [None, None]
    for layer in range(2):
        attn_weights[layer] = gather_attn(layer)
        mlp_weights[layer] = gather_mlp(layer)

    def halves(own, other):
        return ordered(core, own, other, 1)

    def gather_tokens(values):
        two = jnp.concatenate([values, chip_swap(values, 4)], axis=0)
        return jnp.concatenate([two, core_swap(two)], axis=0)

    def reduce_tokens(values):
        two = values[: 2 * tokens] + core_swap(values[2 * tokens :].astype(BF)).astype(F32)
        return two[:tokens] + chip_swap(two[tokens:].astype(BF), 4).astype(F32)

    def forward(layer, rows_in):
        model, qkv_bias, fc_bias = layer_vectors[layer]
        gain_one, bias_one, out_bias, gain_two, bias_two, proj_bias = [model[i] for i in range(6)]
        qkv_own, qkv_other, out_own, out_other = attn_weights[layer]
        fc_weight, proj_weight = mlp_weights[layer]
        normed_float, norm_back_one = jax.vjp(norm_rows, rows_in, gain_one, bias_one)
        normed = normed_float.astype(BF)
        packed = (halves(dot(normed, qkv_own), dot(normed, qkv_other)) + qkv_bias).astype(BF)
        sent = jnp.concatenate([to_slots(packed[:, i * width : (i + 1) * width]) for i in range(3)], axis=2)
        heads_packed = pack_exchange(sent).reshape(PACK_DEVS * tokens, -1)
        heads_ctx, probs = attend(heads_packed, pack_segments)
        context = from_slots(pack_exchange(heads_ctx.reshape(PACK_DEVS, tokens, -1)))
        context = to_own(context)
        attn_out = to_own_wide(halves(dot(context, out_own), dot(context, out_other)))
        middle = rows_in + attn_out + out_bias
        normed_two_float, norm_back_two = jax.vjp(norm_rows, middle, gain_two, bias_two)
        normed_two = gather_tokens(normed_two_float.astype(BF))
        pre_act = dot(normed_two, fc_weight) + fc_bias
        activated = gelu_tanh(pre_act).astype(BF)
        result = middle + reduce_tokens(dot_cols(activated, proj_weight)) + proj_bias
        kept = (norm_back_one, normed, heads_packed, probs, context, norm_back_two, normed_two, pre_act, activated)
        return result, kept

    def plane_terms(rows, columns):
        return [dot_rows(rows[:, k * quarter : (k + 1) * quarter], columns).astype(BF) for k in range(4)]

    def reduce_high(total, last_bit):
        for bit in reversed(range(last_bit, bits)):
            mine = (rank >> bit) & 1
            half = total.shape[0] // 2
            sent = take(total, 1 - mine, half, 0).astype(BF)
            total = take(total, mine, half, 0) + chip_swap(sent, 1 << bit).astype(F32)
        return total

    def backward(layer, upstream, kept):
        norm_back_one, normed, heads_packed, probs, context, norm_back_two, normed_two, pre_act, activated = kept
        qkv_own, qkv_other, out_own, out_other = attn_weights[layer]
        fc_weight, proj_weight = mlp_weights[layer]
        grad_out_low = upstream.astype(BF)
        grad_out_all = gather_tokens(grad_out_low)
        grad_act = dot(grad_out_all, proj_weight)
        gelu_back = jax.vjp(gelu_tanh, pre_act)[1]
        grad_pre = gelu_back(grad_act)[0].astype(BF)
        grad_norm_two = reduce_tokens(dot_cols(grad_pre, fc_weight))
        terms = [
            jnp.concatenate(pair, axis=1)
            for pair in zip(plane_terms(normed_two, grad_pre), plane_terms(grad_out_all, activated))
        ]
        total = reduce_high(reduce_plane(terms).reshape(high, shard, -1), 3)
        small = hidden // 4
        mine = take(total, pair_bit, 1, 0)[0]
        yours = chip_swap(take(total, 1 - pair_bit, 1, 0)[0].astype(BF), 4).astype(F32)
        grad_fc = ordered(pair_bit, mine[:, :small], yours[:, :small], 1)
        grad_proj = ordered(pair_bit, mine[:, small:], yours[:, small:], 1)

        grad_middle_norm, grad_gain_two, grad_bias_two = norm_back_two(grad_norm_two)
        grad_middle = upstream + grad_middle_norm
        grad_attn_own = grad_middle.astype(BF)
        grad_attn = to_natural(grad_attn_own)
        out_half = width // 2
        attn_mine = take(grad_attn, core, out_half, 1)
        attn_yours = take(grad_attn, 1 - core, out_half, 1)
        grad_context = (dot_cols(attn_mine, out_own) + dot_cols(attn_yours, out_other)).astype(BF)
        heads_grad = pack_exchange(to_slots(to_natural(grad_context))).reshape(PACK_DEVS * tokens, -1)
        heads_back = attend_back(heads_packed, probs, heads_grad)
        back = pack_exchange(jnp.concatenate(heads_back, axis=1).reshape(PACK_DEVS, tokens, -1))
        grad_packed = jnp.concatenate(
            [from_slots(back[:, :, i * SLOT_COLS : (i + 1) * SLOT_COLS]) for i in range(3)], axis=1
        )
        qkv_half = 3 * width // 2
        packed_mine = take(grad_packed, core, qkv_half, 1)
        packed_yours = take(grad_packed, 1 - core, qkv_half, 1)
        grad_normed = dot_cols(packed_mine, qkv_own) + dot_cols(packed_yours, qkv_other)
        grad_rows_norm, grad_gain_one, grad_bias_one = norm_back_one(grad_normed)
        grad_rows = grad_middle + grad_rows_norm
        got = core_swap(jnp.concatenate([normed, context, packed_yours, attn_yours], axis=1))
        normed_both = jnp.concatenate([normed, got[:, :width]], axis=0)
        context_both = jnp.concatenate([context, got[:, width : 2 * width]], axis=0)
        packed_both = jnp.concatenate([packed_mine, got[:, 2 * width : 2 * width + qkv_half]], axis=0)
        attn_both = jnp.concatenate([attn_mine, got[:, 2 * width + qkv_half :]], axis=0)
        terms = [
            jnp.concatenate(pair, axis=1)
            for pair in zip(plane_terms(normed_both, packed_both), plane_terms(context_both, attn_both))
        ]
        grad_attn_weights = reduce_high(reduce_plane(terms).reshape(high, shard, -1), 2)[0]
        model = jnp.stack(
            [
                grad_gain_one,
                grad_bias_one,
                jnp.sum(grad_attn_own.astype(F32), axis=0),
                grad_gain_two,
                grad_bias_two,
                jnp.sum(grad_out_low.astype(F32), axis=0),
            ]
        )
        model = lax.dot_general(
            model,
            order.astype(F32),
            (((1,), (1,)), ((), ())),
            precision=lax.Precision.HIGHEST,
            preferred_element_type=F32,
        )
        packed_float = grad_packed.astype(F32)
        qv = jnp.concatenate([jnp.sum(packed_float[:, :width], axis=0), jnp.sum(packed_float[:, 2 * width :], axis=0)])
        fc = lax.dynamic_update_slice_in_dim(
            jnp.zeros((hidden,), F32),
            jnp.sum(grad_pre.astype(F32), axis=0),
            core * (hidden // 2) + pair_bit * small,
            0,
        )
        vector_rows = jnp.concatenate(
            [model[i].reshape(count, shard) for i in range(6)]
            + [qv.reshape(count, 2 * shard), fc.reshape(count, 4 * shard)],
            axis=1,
        )
        return grad_rows, vector_rows, (grad_attn_weights[:, :qkv_half], grad_attn_weights[:, qkv_half:], grad_fc, grad_proj)

    own_inputs = lax.dynamic_index_in_dim(inputs, core, 0, False)
    own_cotangent = lax.dynamic_index_in_dim(cotangent, core, 0, False)
    first_out, first_kept = forward(0, to_own(own_inputs).astype(F32))
    first_low = first_out.astype(BF)
    second_out, second_kept = forward(1, first_low.astype(F32))
    second_low = second_out.astype(BF)
    second_grad, second_vectors, second_mats = backward(1, to_own(own_cotangent).astype(F32), second_kept)
    second_grad_low = second_grad.astype(BF)
    first_grad, first_vectors, first_mats = backward(0, second_grad_low.astype(F32), first_kept)
    first_grad_low = first_grad.astype(BF)

    def by_section(first, second):
        own = jnp.where(core == 0, first, second)
        got = core_swap(jnp.where(core == 0, second, first))
        return ordered(core, own[None], got[None], 0)

    section_outputs = by_section(to_natural(first_low), to_natural(second_low))
    input_grads = by_section(to_natural(first_grad_low), to_natural(second_grad_low))

    mats = []
    for first, second in zip(first_mats, second_mats):
        own = jnp.where(core == 0, first, second)
        got = core_swap(jnp.where(core == 0, second, first))
        mats.append(ordered(core, own, got, 1))
    vector_rows = jnp.where(core == 0, first_vectors, second_vectors) + core_swap(
        jnp.where(core == 0, second_vectors, first_vectors)
    )
    vector_own = reduce_vector(vector_rows)
    model = [vector_own[i * shard : (i + 1) * shard] for i in range(6)]
    return (
        section_outputs[None],
        input_grads[None],
        model[0][None],
        model[1][None],
        mats[0][None],
        vector_own[6 * shard : 8 * shard][None],
        mats[1][None],
        model[2][None],
        model[3][None],
        model[4][None],
        mats[2][None],
        vector_own[8 * shard :][None],
        mats[3][None],
        model[5][None],
    )


def solution(mesh):
    in_specs = (
        P(None, "fsdp", None),
        P(None, "fsdp", None),
        P(None, "fsdp"),
        P("section", "fsdp"),
        P("section", "fsdp"),
        P("section", "fsdp", None),
        P("section", "fsdp"),
        P("section", "fsdp", None),
        P("section", "fsdp"),
        P("section", "fsdp"),
        P("section", "fsdp"),
        P("section", "fsdp", None),
        P("section", "fsdp"),
        P("section", "fsdp", None),
        P("section", "fsdp"),
    )
    out_specs = (
        P("section", None, "fsdp", None),
        P("section", None, "fsdp", None),
        P("section", "fsdp"),
        P("section", "fsdp"),
        P("section", "fsdp", None),
        P("section", "fsdp"),
        P("section", "fsdp", None),
        P("section", "fsdp"),
        P("section", "fsdp"),
        P("section", "fsdp"),
        P("section", "fsdp", None),
        P("section", "fsdp"),
        P("section", "fsdp", None),
        P("section", "fsdp"),
    )
    return jax.shard_map(
        on_device, mesh=mesh, in_specs=in_specs, out_specs=out_specs, check_vma=False
    )
```

time: 6680 us -> 1450 us (0.22)
  waiting for transfers between devices: 4760 us -> 601 us
  starting transfers between devices: 770 us -> 171 us
  matrix products: 526 us -> 224 us
  blocking collectives: 149 us -> 0 us
  local copies, waits for them, and re-layouts: 337 us -> 200 us
  other arithmetic: 102 us -> 187 us
    unnamed x8 -> x0, waiting for transfers between devices: 3040 us -> none
    all_gather x4 -> x0, waiting for transfers between devices: 1070 us -> none  [the longest x1 397 us: fetch_weights(): lax.all_gather(w_fc, 'fsdp', axis=1, tiled=True)]
    ppermute x67 -> x92, starting transfers between devices: 769 us -> 110 us  [the longest x64 107 us: chip_swap(): return lax.ppermute(value, 'fsdp', [(i, i ^ mask) for i in range(count)])]
    dot_general x53 -> x74, matrix products: 458 us -> 224 us  [the longest x22 92.2 us: dot(): return jnp.dot(left, right, preferred_element_type=F32)]
    concatenate x8 -> x21, local copies, waits for them, and re-layouts: 144 us -> 17.8 us  [the longest x2 5.75 us: forward(): jnp.concatenate([to_slots(packed[:, i * width:(i + 1) * width]) for i in...]
    ppermute x67 -> x92, waiting for transfers between devices: 658 us -> 559 us  [the longest x64 558 us: chip_swap(): return lax.ppermute(value, 'fsdp', [(i, i ^ mask) for i in range(count)])]
    unnamed x498 -> x398, local copies, waits for them, and re-layouts: 144 us -> 50.4 us
    concatenate x0 -> x38, other arithmetic: none -> 83.5 us  [the longest x2 25.2 us: gather_mlp(): full = jnp.concatenate(gather_plane(rows), axis=0)]
  transfers between devices with their start and end apart: 73 -> 100, of which waited for: 39 -> 31; matrix products, arithmetic and copies ran while one was open for 6% -> 41% of each run, Pallas kernels for 0% -> 3%
where the time goes in v1:
time: 1450 us; the launch traced here: 1430 us
  waiting for transfers between devices  601 us (41%)
  matrix products  224 us (15%)
  local copies, waits for them, and re-layouts  200 us (14%)
  other arithmetic  187 us (13%)
  starting transfers between devices  171 us (12%)
  Pallas kernels  48.1 us (3%)
    ppermute x64, waiting for transfers between devices, chip_swap(): return lax.ppermute(value, 'fsdp', [(i, i ^ mask) for i in range(count)])  558 us
    ppermute x64, starting transfers between devices, chip_swap(): return lax.ppermute(value, 'fsdp', [(i, i ^ mask) for i in range(count)])  107 us
    dot_general x22, matrix products, dot(): return jnp.dot(left, right, preferred_element_type=F32)  92.2 us
    dot_general x18, matrix products, dot_cols(): lax.dot_general(left, right, (((1,), (1,)), ((), ())), preferred_element_...  67.9 us
    all_to_all x8, starting transfers between devices, pack_exchange(): return lax.all_to_all(value, 'fsdp', 0, 0, axis_index_groups=groups)  60.1 us
    dot_general x32, matrix products, dot_rows(): lax.dot_general(left, right, (((0,), (0,)), ((), ())), preferred_element_...  52.6 us
    unnamed x398, local copies, waits for them, and re-layouts  50.4 us
    all_to_all x8, waiting for transfers between devices, pack_exchange(): return lax.all_to_all(value, 'fsdp', 0, 0, axis_index_groups=groups)  42.3 us
  transfers between devices with their start and end apart: 100, of which 31 were waited for; matrix products, arithmetic and copies ran while one was open for 41% of the time, Pallas kernels for 3%

profile of v1, /device:TPU:0, one launch (start us, length us, event | category | flops | bytes accessed | tf_op | source)
XLA Modules:
  0.0 1434.2 jit_solution(12661232412625952897)
XLA Ops:
  46.7 14.5 %collective-permute-done.6 = bf16[1,100,3200]{2,1,0:T(8,128)(2,1)S(1)} collective-permute-done((bf16[1,100,3200]{2,1,0:T(8,128)(2,1)S(1)}, bf16[1,100,3200]{2,1,0:T(8,128)(2,1)S(1)}, u32[]{:S(2)}, u32[]{:S(2)}) %collective-permute-start.6) | collective-permute-done | bytes 640032 | tf_op jit(solution)/shard_map/ppermute | solution.py:24
  68.3 51.5 %collective-permute-done.7 = bf16[2,100,3200]{2,0,1:T(2,128)(2,1)S(1)} collective-permute-done((bf16[2,100,3200]{2,0,1:T(2,128)(2,1)S(1)}, bf16[2,100,3200]{2,0,1:T(2,128)(2,1)S(1)}, u32[]{:S(2)}, u32[]{:S(2)}) %collective-permute-start.7) | collective-permute-done | bytes 1280032 | tf_op jit(solution)/shard_map/ppermute | solution.py:24
  139.2 41.8 %collective-permute-done.9 = bf16[400,3200]{1,0:T(8,128)(2,1)} collective-permute-done((bf16[400,3200]{1,0:T(8,128)(2,1)}, bf16[400,3200]{1,0:T(8,128)(2,1)}, u32[]{:S(2)}, u32[]{:S(2)}) %collective-permute-start.9) | collective-permute-done | bytes 2560032 | tf_op jit(solution)/shard_map/ppermute | solution.py:24
  248.0 18.0 %all-to-all-start = ((bf16[8,128,768]{2,1,0:T(8,128)(2,1)}), bf16[8,128,768]{2,1,0:T(8,128)(2,1)S(1)}, u32[]{:S(2)}, u32[]{:S(2)}) async-start(bf16[8,128,768]{2,1,0:T(8,128)(2,1)} %concatenate.611), calls=%async_computation | async-start | bytes 3145728 | tf_op jit(solution)/shard_map/all_to_all | solution.py:188
  281.8 18.1 %collective-permute-done.30 = bf16[400,3200]{1,0:T(8,128)(2,1)} collective-permute-done((bf16[400,3200]{1,0:T(8,128)(2,1)}, bf16[400,3200]{1,0:T(8,128)(2,1)}, u32[]{:S(2)}, u32[]{:S(2)}) %collective-permute-start.30) | collective-permute-done | bytes 2560032 | tf_op jit(solution)/shard_map/ppermute | solution.py:24
  320.2 18.0 %all-to-all-start.1 = ((bf16[8,128,256]{1,2,0:T(8,128)(2,1)}), bf16[8,128,256]{1,2,0:T(8,128)(2,1)S(1)}, u32[]{:S(2)}, u32[]{:S(2)}) async-start(bf16[8,128,256]{1,2,0:T(8,128)(2,1)} %copy.132), calls=%async_computation.1 | async-start | bytes 1048576 | tf_op jit(solution)/shard_map/all_to_all | solution.py:188
  343.7 18.2 %collective-permute-done.22 = bf16[400,3200]{1,0:T(8,128)(2,1)} collective-permute-done((bf16[400,3200]{1,0:T(8,128)(2,1)}, bf16[400,3200]{1,0:T(8,128)(2,1)}, u32[]{:S(2)}, u32[]{:S(2)}) %collective-permute-start.22) | collective-permute-done | bytes 2560032 | tf_op jit(solution)/shard_map/ppermute | solution.py:24
  374.6 17.2 %collective-permute-done.31 = bf16[400,1600]{1,0:T(8,128)(2,1)} collective-permute-done((bf16[400,1600]{1,0:T(8,128)(2,1)}, bf16[400,1600]{1,0:T(8,128)(2,1)}, u32[]{:S(2)}, u32[]{:S(2)}) %collective-permute-start.31) | collective-permute-done | bytes 1280032 | tf_op jit(solution)/shard_map/ppermute | solution.py:24
  412.1 16.4 %collective-permute-start.16 = (bf16[128,1600]{0,1:T(8,128)(2,1)S(1)}, bf16[128,1600]{0,1:T(8,128)(2,1)S(1)}, u32[]{:S(2)}, u32[]{:S(2)}) collective-permute-start(bf16[128,1600]{0,1:T(8,128)(2,1)S(1)} %add_convert_fusion.7), channel_id=1, source_target_pairs={{0,4},{1,5},{2,6},{3,7},{4,0},{5,1},{6,2},{7,3},{8,12},{9,13},{10,... | collective-permute-start | bytes 1228808 | tf_op jit(solution)/shard_map/ppermute | solution.py:24
  438.3 12.4 fusion.21
  517.4 55.4 %collective-permute-done.40 = bf16[2,100,3200]{2,0,1:T(2,128)(2,1)S(1)} collective-permute-done((bf16[2,100,3200]{2,0,1:T(2,128)(2,1)S(1)}, bf16[2,100,3200]{2,0,1:T(2,128)(2,1)S(1)}, u32[]{:S(2)}, u32[]{:S(2)}) %collective-permute-start.40) | collective-permute-done | bytes 1280032 | tf_op jit(solution)/shard_map/ppermute | solution.py:24
  608.2 30.5 %collective-permute-done.42 = bf16[400,3200]{1,0:T(8,128)(2,1)} collective-permute-done((bf16[400,3200]{1,0:T(8,128)(2,1)}, bf16[400,3200]{1,0:T(8,128)(2,1)}, u32[]{:S(2)}, u32[]{:S(2)}) %collective-permute-start.42) | collective-permute-done | bytes 2560032 | tf_op jit(solution)/shard_map/ppermute | solution.py:24
  681.7 12.8 fusion.20
  788.2 13.0 shard_map.256
  820.1 26.8 %collective-permute-done.87 = bf16[400,3200]{1,0:T(8,128)(2,1)} collective-permute-done((bf16[400,3200]{1,0:T(8,128)(2,1)}, bf16[400,3200]{1,0:T(8,128)(2,1)}, u32[]{:S(2)}, u32[]{:S(2)}) %collective-permute-start.87) | collective-permute-done | bytes 2560032 | tf_op jit(solution)/shard_map/ppermute | solution.py:24
  925.7 13.1 collective-permute-done.89
  1030.7 12.9 shard_map.257
  1054.7 40.4 %collective-permute-done.81 = bf16[400,3200]{1,0:T(8,128)(2,1)} collective-permute-done((bf16[400,3200]{1,0:T(8,128)(2,1)}, bf16[400,3200]{1,0:T(8,128)(2,1)}, u32[]{:S(2)}, u32[]{:S(2)}) %collective-permute-start.81) | collective-permute-done | bytes 2560032 | tf_op jit(solution)/shard_map/ppermute | solution.py:24
  1112.2 42.3 %all-to-all-done.7 = bf16[8,128,768]{1,2,0:T(8,128)(2,1)S(1)} async-done(((bf16[8,128,768]{1,2,0:T(8,128)(2,1)}), bf16[8,128,768]{1,2,0:T(8,128)(2,1)S(1)}, u32[]{:S(2)}, u32[]{:S(2)}) %all-to-all-start.7) | async-done | bytes 1572896 | tf_op jit(solution)/shard_map/all_to_all | solution.py:188
  1201.6 26.7 %collective-permute-done.59 = f32[4,1200]{1,0:T(4,128)S(1)} collective-permute-done((f32[4,1200]{1,0:T(4,128)S(1)}, f32[4,1200]{1,0:T(4,128)S(1)}, u32[]{:S(2)}, u32[]{:S(2)}) %collective-permute-start.59) | collective-permute-done | bytes 19232 | tf_op jit(solution)/shard_map/ppermute | solution.py:24
  1250.0 25.1 %collective-permute-done.65 = bf16[400,1600]{1,0:T(8,128)(2,1)S(1)} collective-permute-done((bf16[400,1600]{1,0:T(8,128)(2,1)S(1)}, bf16[400,1600]{1,0:T(8,128)(2,1)S(1)}, u32[]{:S(2)}, u32[]{:S(2)}) %collective-permute-start.65) | collective-permute-done | bytes 1280032 | tf_op jit(solution)/shard_map/ppermute | solution.py:24
  1286.8 46.3 %collective-permute-done.66 = bf16[400,3200]{1,0:T(8,128)(2,1)S(1)} collective-permute-done((bf16[400,3200]{1,0:T(8,128)(2,1)S(1)}, bf16[400,3200]{1,0:T(8,128)(2,1)S(1)}, u32[]{:S(2)}, u32[]{:S(2)}) %collective-permute-start.66) | collective-permute-done | bytes 2560032 | tf_op jit(solution)/shard_map/ppermute | solution.py:24
  1351.1 50.7 %collective-permute-done.67 = bf16[2,100,3200]{2,0,1:T(2,128)(2,1)S(1)} collective-permute-done((bf16[2,100,3200]{2,0,1:T(2,128)(2,1)S(1)}, bf16[2,100,3200]{2,0,1:T(2,128)(2,1)S(1)}, u32[]{:S(2)}, u32[]{:S(2)}) %collective-permute-start.67) | collective-permute-done | bytes 1280032 | tf_op jit(solution)/shard_map/ppermute | solution.py:24
  1404.6 13.9 collective-permute-done.68
  (983 shorter events, 793.9 us)
Async XLA Ops:
  46.2 83.5 %collective-permute-start.27 = (bf16[1,100,3200]{2,1,0:T(8,128)(2,1)}, bf16[1,100,3200]{2,1,0:T(8,128)(2,1)}, u32[]{:S(2)}, u32[]{:S(2)}) collective-permute-start(bf16[1,100,3200]{2,1,0:T(8,128)(2,1)} %get-tuple-element.168), channel_id=1, source_target_pairs={{0,4},{1,5},{2,6},{3,7},{4,0},{5,1},{6,2},{7,3},{8,12},{9,13},{10,... | collective-permute-start | bytes 1920008 | tf_op jit(solution)/shard_map/ppermute | solution.py:24
  127.7 74.0 %collective-permute-start.12 = (bf16[400,3200]{1,0:T(8,128)(2,1)}, bf16[400,3200]{1,0:T(8,128)(2,1)}, u32[]{:S(2)}, u32[]{:S(2)}) collective-permute-start(bf16[400,3200]{1,0:T(8,128)(2,1)} %select_n.549), channel_id=1, source_target_pairs={{0,16},{16,0},{1,17},{17,1},{2,18},{18,2},{3,19},{19,3},{4,20},{20... | collective-permute-start | bytes 7680008 | tf_op jit(solution)/shard_map/ppermute | solution.py:28
  193.8 75.0 %collective-permute-start.20 = (bf16[2,100,3200]{2,0,1:T(2,128)(2,1)}, bf16[2,100,3200]{2,0,1:T(2,128)(2,1)}, u32[]{:S(2)}, u32[]{:S(2)}) collective-permute-start(bf16[2,100,3200]{2,0,1:T(2,128)(2,1)} %copy.133), channel_id=1, source_target_pairs={{0,8},{1,9},{2,10},{3,11},{4,12},{5,13},{6,14},{7,15},{8,0},{9,1},... | collective-permute-start | bytes 3840008 | tf_op jit(solution)/shard_map/ppermute | solution.py:24
  200.2 103.8 %collective-permute-start.29 = (bf16[400,3200]{1,0:T(8,128)(2,1)}, bf16[400,3200]{1,0:T(8,128)(2,1)}, u32[]{:S(2)}, u32[]{:S(2)}) collective-permute-start(bf16[400,3200]{1,0:T(8,128)(2,1)} %select_n.570), channel_id=1, source_target_pairs={{0,1},{1,0},{2,3},{3,2},{4,5},{5,4},{6,7},{7,6},{8,9},{9,8},{10,11... | collective-permute-start | bytes 7680008 | tf_op jit(solution)/shard_map/ppermute | solution.py:24
  228.7 71.3 %collective-permute-start.30 = (bf16[400,3200]{1,0:T(8,128)(2,1)}, bf16[400,3200]{1,0:T(8,128)(2,1)}, u32[]{:S(2)}, u32[]{:S(2)}) collective-permute-start(bf16[400,3200]{1,0:T(8,128)(2,1)} %select_n.570), channel_id=1, source_target_pairs={{0,2},{1,3},{2,0},{3,1},{4,6},{5,7},{6,4},{7,5},{8,10},{9,11},{10,... | collective-permute-start | bytes 7680008 | tf_op jit(solution)/shard_map/ppermute | solution.py:24
  268.8 69.4 %collective-permute-start.33 = (bf16[400,3200]{1,0:T(8,128)(2,1)}, bf16[400,3200]{1,0:T(8,128)(2,1)}, u32[]{:S(2)}, u32[]{:S(2)}) collective-permute-start(bf16[400,3200]{1,0:T(8,128)(2,1)} %select_n.570), channel_id=1, source_target_pairs={{0,16},{16,0},{1,17},{17,1},{2,18},{18,2},{3,19},{19,3},{4,20},{20... | collective-permute-start | bytes 7680008 | tf_op jit(solution)/shard_map/ppermute | solution.py:28
  275.3 86.6 %collective-permute-start.22 = (bf16[400,3200]{1,0:T(8,128)(2,1)}, bf16[400,3200]{1,0:T(8,128)(2,1)}, u32[]{:S(2)}, u32[]{:S(2)}) collective-permute-start(bf16[400,3200]{1,0:T(8,128)(2,1)} %select_n.562), channel_id=1, source_target_pairs={{0,2},{1,3},{2,0},{3,1},{4,6},{5,7},{6,4},{7,5},{8,10},{9,11},{10,... | collective-permute-start | bytes 7680008 | tf_op jit(solution)/shard_map/ppermute | solution.py:24
  277.3 87.5 %collective-permute-start.21 = (bf16[400,3200]{1,0:T(8,128)(2,1)}, bf16[400,3200]{1,0:T(8,128)(2,1)}, u32[]{:S(2)}, u32[]{:S(2)}) collective-permute-start(bf16[400,3200]{1,0:T(8,128)(2,1)} %select_n.562), channel_id=1, source_target_pairs={{0,1},{1,0},{2,3},{3,2},{4,5},{5,4},{6,7},{7,6},{8,9},{9,8},{10,11... | collective-permute-start | bytes 7680008 | tf_op jit(solution)/shard_map/ppermute | solution.py:24
  302.9 70.1 %collective-permute-start.32 = (bf16[400,1600]{1,0:T(8,128)(2,1)}, bf16[400,1600]{1,0:T(8,128)(2,1)}, u32[]{:S(2)}, u32[]{:S(2)}) collective-permute-start(bf16[400,1600]{1,0:T(8,128)(2,1)} %slice.894), channel_id=1, source_target_pairs={{0,1},{1,0},{2,3},{3,2},{4,5},{5,4},{6,7},{7,6},{8,9},{9,8},{10,11... | collective-permute-start | bytes 3840008 | tf_op jit(solution)/shard_map/ppermute | solution.py:24
  306.5 85.2 %collective-permute-start.31 = (bf16[400,1600]{1,0:T(8,128)(2,1)}, bf16[400,1600]{1,0:T(8,128)(2,1)}, u32[]{:S(2)}, u32[]{:S(2)}) collective-permute-start(bf16[400,1600]{1,0:T(8,128)(2,1)} %slice.893), channel_id=1, source_target_pairs={{0,2},{1,3},{2,0},{3,1},{4,6},{5,7},{6,4},{7,5},{8,10},{9,11},{10,... | collective-permute-start | bytes 3840008 | tf_op jit(solution)/shard_map/ppermute | solution.py:24
  320.2 75.4 %all-to-all-start.1 = ((bf16[8,128,256]{1,2,0:T(8,128)(2,1)}), bf16[8,128,256]{1,2,0:T(8,128)(2,1)S(1)}, u32[]{:S(2)}, u32[]{:S(2)}) async-start(bf16[8,128,256]{1,2,0:T(8,128)(2,1)} %copy.132), calls=%async_computation.1 | async-start | bytes 1048576 | tf_op jit(solution)/shard_map/all_to_all | solution.py:188
  338.2 172.7 %collective-permute-start.39 = (bf16[100,3200]{1,0:T(8,128)(2,1)}, bf16[100,3200]{1,0:T(8,128)(2,1)}, u32[]{:S(2)}, u32[]{:S(2)}) collective-permute-start(bf16[100,3200]{1,0:T(8,128)(2,1)} %pad_maximum_fusion.37), channel_id=1, source_target_pairs={{0,4},{1,5},{2,6},{3,7},{4,0},{5,1},{6,2},{7,3},{8,12},{9,13},{10,... | collective-permute-start | bytes 1920008 | tf_op jit(solution)/shard_map/ppermute | solution.py:24
  361.9 100.2 %collective-permute-start.34 = (bf16[400,3200]{1,0:T(8,128)(2,1)}, bf16[400,3200]{1,0:T(8,128)(2,1)}, u32[]{:S(2)}, u32[]{:S(2)}) collective-permute-start(bf16[400,3200]{1,0:T(8,128)(2,1)} %collective-permute-done.29), channel_id=1, source_target_pairs={{0,16},{16,0},{1,17},{17,1},{2,18},{18,2},{3,19},{19,3},{4,20},{20... | collective-permute-start | bytes 7680008 | tf_op jit(solution)/shard_map/ppermute | solution.py:28
  364.8 73.0 %collective-permute-start.24 = (bf16[400,1600]{1,0:T(8,128)(2,1)}, bf16[400,1600]{1,0:T(8,128)(2,1)}, u32[]{:S(2)}, u32[]{:S(2)}) collective-permute-start(bf16[400,1600]{1,0:T(8,128)(2,1)} %slice.874), channel_id=1, source_target_pairs={{0,1},{1,0},{2,3},{3,2},{4,5},{5,4},{6,7},{7,6},{8,9},{9,8},{10,11... | collective-permute-start | bytes 3840008 | tf_op jit(solution)/shard_map/ppermute | solution.py:24
  506.9 79.8 %all-to-all-start.2 = ((bf16[8,128,768]{2,1,0:T(8,128)(2,1)}), bf16[8,128,768]{2,1,0:T(8,128)(2,1)S(1)}, u32[]{:S(2)}, u32[]{:S(2)}) async-start(bf16[8,128,768]{2,1,0:T(8,128)(2,1)} %concatenate.640), calls=%async_computation.2 | async-start | bytes 3145728 | tf_op jit(solution)/shard_map/all_to_all | solution.py:188
  1018.0 77.1 %collective-permute-start.81 = (bf16[400,3200]{1,0:T(8,128)(2,1)}, bf16[400,3200]{1,0:T(8,128)(2,1)}, u32[]{:S(2)}, u32[]{:S(2)}) collective-permute-start(bf16[400,3200]{1,0:T(8,128)(2,1)} %pad_maximum_fusion.11), channel_id=1, source_target_pairs={{0,2},{1,3},{2,0},{3,1},{4,6},{5,7},{6,4},{7,5},{8,10},{9,11},{10,... | collective-permute-start | bytes 7680008 | tf_op jit(solution)/shard_map/ppermute | solution.py:24
  1024.5 70.6 %collective-permute-start.79 = (bf16[400,3200]{1,0:T(8,128)(2,1)}, bf16[400,3200]{1,0:T(8,128)(2,1)}, u32[]{:S(2)}, u32[]{:S(2)}) collective-permute-start(bf16[400,3200]{1,0:T(8,128)(2,1)} %pad_maximum_fusion.10), channel_id=1, source_target_pairs={{0,1},{1,0},{2,3},{3,2},{4,5},{5,4},{6,7},{7,6},{8,9},{9,8},{10,11... | collective-permute-start | bytes 7680008 | tf_op jit(solution)/shard_map/ppermute | solution.py:24
  1030.2 152.0 %collective-permute-start.73 = (bf16[400,3200]{1,0:T(8,128)(2,1)}, bf16[400,3200]{1,0:T(8,128)(2,1)}, u32[]{:S(2)}, u32[]{:S(2)}) collective-permute-start(bf16[400,3200]{1,0:T(8,128)(2,1)} %pad_maximum_fusion.9), channel_id=1, source_target_pairs={{0,2},{1,3},{2,0},{3,1},{4,6},{5,7},{6,4},{7,5},{8,10},{9,11},{10,... | collective-permute-start | bytes 7680008 | tf_op jit(solution)/shard_map/ppermute | solution.py:24
  1045.3 109.1 %all-to-all-start.7 = ((bf16[8,128,768]{1,2,0:T(8,128)(2,1)}), bf16[8,128,768]{1,2,0:T(8,128)(2,1)S(1)}, u32[]{:S(2)}, u32[]{:S(2)}) async-start(bf16[8,128,768]{1,2,0:T(8,128)(2,1)} %copy.155), calls=%async_computation.7 | async-start | bytes 3145728 | tf_op jit(solution)/shard_map/all_to_all | solution.py:188
  1052.7 129.5 %collective-permute-start.71 = (bf16[400,3200]{1,0:T(8,128)(2,1)}, bf16[400,3200]{1,0:T(8,128)(2,1)}, u32[]{:S(2)}, u32[]{:S(2)}) collective-permute-start(bf16[400,3200]{1,0:T(8,128)(2,1)} %fusion.115), channel_id=1, source_target_pairs={{0,1},{1,0},{2,3},{3,2},{4,5},{5,4},{6,7},{7,6},{8,9},{9,8},{10,11... | collective-permute-start | bytes 7680008 | tf_op jit(solution)/shard_map/ppermute | solution.py:24
  1109.7 128.0 %collective-permute-start.82 = (bf16[2,100,3200]{2,0,1:T(2,128)(2,1)}, bf16[2,100,3200]{2,0,1:T(2,128)(2,1)}, u32[]{:S(2)}, u32[]{:S(2)}) collective-permute-start(bf16[2,100,3200]{2,0,1:T(2,128)(2,1)} %copy.189), channel_id=1, source_target_pairs={{0,8},{1,9},{2,10},{3,11},{4,12},{5,13},{6,14},{7,15},{8,0},{9,1},... | collective-permute-start | bytes 3840008 | tf_op jit(solution)/shard_map/ppermute | solution.py:24
  1199.4 80.2 %collective-permute-start.74 = (bf16[2,100,3200]{2,0,1:T(2,128)(2,1)S(1)}, bf16[2,100,3200]{2,0,1:T(2,128)(2,1)S(1)}, u32[]{:S(2)}, u32[]{:S(2)}) collective-permute-start(bf16[2,100,3200]{2,0,1:T(2,128)(2,1)S(1)} %copy.190), channel_id=1, source_target_pairs={{0,8},{1,9},{2,10},{3,11},{4,12},{5,13},{6,14},{7,15},{8,0},{9,1},... | collective-permute-start | bytes 3840008 | tf_op jit(solution)/shard_map/ppermute | solution.py:24
  1285.6 117.0 %collective-permute-start.90 = (f32[100,3200]{1,0:T(8,128)}, f32[100,3200]{1,0:T(8,128)}, u32[]{:S(2)}, u32[]{:S(2)}) collective-permute-start(f32[100,3200]{1,0:T(8,128)} %get-tuple-element.147), channel_id=1, source_target_pairs={{0,16},{16,0},{1,17},{17,1},{2,18},{18,2},{3,19},{19,3},{4,20},{20... | collective-permute-start | bytes 3840008 | tf_op jit(solution)/shard_map/ppermute | solution.py:28
  1349.0 70.6 %collective-permute-start.91 = (f32[100,3200]{1,0:T(8,128)S(1)}, f32[100,3200]{1,0:T(8,128)S(1)}, u32[]{:S(2)}, u32[]{:S(2)}) collective-permute-start(f32[100,3200]{1,0:T(8,128)S(1)} %get-tuple-element.145), channel_id=1, source_target_pairs={{0,16},{16,0},{1,17},{17,1},{2,18},{18,2},{3,19},{19,3},{4,20},{20... | collective-permute-start | bytes 3840008 | tf_op jit(solution)/shard_map/ppermute | solution.py:28
  (260 other events, 5824.2 us)

commit v2 on v1

v2 whole, which is shorter than its diff:
```python
import math

import jax
import jax.numpy as jnp
from jax import lax
from jax.experimental import pallas as pl
from jax.experimental.pallas import tpu as pltpu
from jax.sharding import PartitionSpec as P

HEADS = 25
HEAD_DIM = 64
SEQ_LEN = 1024
PACK_DEVS = 8
MAIN = HEADS // PACK_DEVS
SLOTS = 4
SLOT_COLS = SLOTS * HEAD_DIM
BLOCK = 256
BF = jnp.bfloat16
F32 = jnp.float32


def chip_swap(value, mask):
    count = lax.axis_size("fsdp")
    return lax.ppermute(value, "fsdp", [(i, i ^ mask) for i in range(count)])


def core_swap(value):
    return lax.ppermute(value, "section", [(0, 1), (1, 0)])


def fence(*values):
    return lax.optimization_barrier(values)


def ordered(bit, own, other, axis):
    return jnp.where(
        bit == 0,
        jnp.concatenate([own, other], axis=axis),
        jnp.concatenate([other, own], axis=axis),
    )


def take(value, index, size, axis):
    return lax.dynamic_slice_in_dim(value, index * size, size, axis)


def dot(left, right):
    return jnp.dot(left, right, preferred_element_type=F32)


def dot_rows(left, right):
    return lax.dot_general(left, right, (((0,), (0,)), ((), ())), preferred_element_type=F32)


def dot_cols(left, right):
    return lax.dot_general(left, right, (((1,), (1,)), ((), ())), preferred_element_type=F32)


def norm_rows(values, gain_vec, bias_vec):
    row_mean = jnp.mean(values, axis=-1, keepdims=True)
    centered = values - row_mean
    variance = jnp.mean(centered * centered, axis=-1, keepdims=True)
    return centered * lax.rsqrt(variance + 1e-05) * gain_vec + bias_vec


def gelu_tanh(values):
    return jax.nn.gelu(values, approximate=True)


def tokens_of(ref, first_row, blocks):
    rows = slice(first_row, first_row + HEAD_DIM)
    return jnp.concatenate([ref[s, rows, :] for s in range(blocks)], axis=1)


def attend_kernel(q_ref, k_ref, v_ref, srow_ref, scol_ref, ctx_ref, p_ref, bias_ref):
    per = q_ref.shape[2]
    length = q_ref.shape[0] * per
    step = BLOCK // per

    @pl.when(pl.program_id(0) == 0)
    def _():
        for first in range(0, length, BLOCK):
            wide = first + BLOCK
            key = lax.broadcasted_iota(jnp.int32, (wide, BLOCK), 0)
            query = lax.broadcasted_iota(jnp.int32, (wide, BLOCK), 1) + first
            same = scol_ref[:wide, :] == srow_ref[:, first:wide]
            bias_ref[:wide, first:wide] = jnp.where(same & (key <= query), 0.0, -1e30)

    for h in range(2):
        row = h * HEAD_DIM
        keys = tokens_of(k_ref, row, length // per)
        values = tokens_of(v_ref, row, length // per)
        queries = tokens_of(q_ref, row, length // per) * jnp.asarray(1.0 / math.sqrt(HEAD_DIM), BF)
        for first in range(0, length, BLOCK):
            wide = first + BLOCK
            s = dot_rows(keys[:, :wide], queries[:, first:wide]) + bias_ref[:wide, first:wide]
            m = jnp.max(s, axis=0, keepdims=True)
            e = jnp.exp(s - m)
            p = (e * (1.0 / jnp.sum(e, axis=0, keepdims=True))).astype(BF)
            p_ref[h, :wide, first:wide] = p
            ctx = dot(values[:, :wide], p).astype(BF)
            for i in range(step):
                ctx_ref[first // per + i, row : row + HEAD_DIM, :] = ctx[:, i * per : (i + 1) * per]


def attend_back_kernel(q_ref, k_ref, v_ref, p_ref, d_ref, back_ref, dk_sum, dv_sum):
    per = q_ref.shape[2]
    length = q_ref.shape[0] * per
    step = BLOCK // per
    scale = jnp.asarray(1.0 / math.sqrt(HEAD_DIM), BF)
    for h in range(2):
        row = h * HEAD_DIM
        rows = slice(row, row + HEAD_DIM)
        keys = tokens_of(k_ref, row, length // per) * scale
        values = tokens_of(v_ref, row, length // per)
        queries = tokens_of(q_ref, row, length // per) * scale
        grads = tokens_of(d_ref, row, length // per)
        for first in reversed(range(0, length, BLOCK)):
            wide = first + BLOCK
            d = grads[:, first:wide]
            p_low = p_ref[h, :wide, first:wide]
            dp = dot_rows(values[:, :wide], d)
            p = p_low.astype(F32)
            ds = (p * (dp - jnp.sum(p * dp, axis=0, keepdims=True))).astype(BF)
            dq = dot(keys[:, :wide], ds).astype(BF)
            for i in range(step):
                back_ref[first // per + i, 0, rows, :] = dq[:, i * per : (i + 1) * per]
            dk = dot_cols(queries[:, first:wide], ds)
            dv = dot_cols(d, p_low)
            if wide == length:
                dk_sum[...] = dk
                dv_sum[...] = dv
            else:
                dk_sum[:, :wide] += dk
                dv_sum[:, :wide] += dv
        for s in range(length // per):
            back_ref[s, 1, rows, :] = dk_sum[:, s * per : (s + 1) * per].astype(BF)
            back_ref[s, 2, rows, :] = dv_sum[:, s * per : (s + 1) * per].astype(BF)


def attend(packed, segs):
    devices, _, per = packed.shape
    length = devices * per
    pairs = SLOTS // 2
    rows = 2 * HEAD_DIM
    return pl.pallas_call(
        attend_kernel,
        grid=(pairs,),
        in_specs=[
            pl.BlockSpec((devices, rows, per), lambda g: (0, g, 0)),
            pl.BlockSpec((devices, rows, per), lambda g: (0, pairs + g, 0)),
            pl.BlockSpec((devices, rows, per), lambda g: (0, 2 * pairs + g, 0)),
            pl.BlockSpec((1, length), lambda g: (0, 0)),
            pl.BlockSpec((length, 1), lambda g: (0, 0)),
        ],
        out_specs=[
            pl.BlockSpec((devices, rows, per), lambda g: (0, g, 0)),
            pl.BlockSpec((2, length, length), lambda g: (g, 0, 0)),
        ],
        out_shape=[
            jax.ShapeDtypeStruct((devices, SLOT_COLS, per), BF),
            jax.ShapeDtypeStruct((SLOTS, length, length), BF),
        ],
        scratch_shapes=[pltpu.VMEM((length, length), F32)],
        compiler_params=pltpu.CompilerParams(vmem_limit_bytes=48 * 1024 * 1024),
        cost_estimate=pl.CostEstimate(flops=12 * 10**9, bytes_accessed=12 * 10**6, transcendentals=0),
    )(packed, packed, packed, segs.reshape(1, length), segs.reshape(length, 1))


def attend_back(packed, probs, grad):
    devices, _, per = packed.shape
    length = devices * per
    pairs = SLOTS // 2
    rows = 2 * HEAD_DIM
    pair_block = pl.BlockSpec((devices, rows, per), lambda g: (0, g, 0))
    back = pl.pallas_call(
        attend_back_kernel,
        grid=(pairs,),
        in_specs=[
            pair_block,
            pl.BlockSpec((devices, rows, per), lambda g: (0, pairs + g, 0)),
            pl.BlockSpec((devices, rows, per), lambda g: (0, 2 * pairs + g, 0)),
            pl.BlockSpec((2, length, length), lambda g: (g, 0, 0)),
            pair_block,
        ],
        out_specs=pl.BlockSpec((devices, 3, rows, per), lambda g: (0, 0, g, 0)),
        out_shape=jax.ShapeDtypeStruct((devices, 3, SLOT_COLS, per), BF),
        scratch_shapes=[pltpu.VMEM((HEAD_DIM, length), F32)] * 2,
        compiler_params=pltpu.CompilerParams(vmem_limit_bytes=48 * 1024 * 1024),
        cost_estimate=pl.CostEstimate(flops=24 * 10**9, bytes_accessed=12 * 10**6, transcendentals=0),
    )(packed, packed, packed, probs, grad)
    return back.reshape(devices, 3 * SLOT_COLS, per)


def to_slots(values):
    split = PACK_DEVS * MAIN * HEAD_DIM
    main = values[:split].reshape(PACK_DEVS, MAIN * HEAD_DIM, -1)
    last = values[None, split:]
    none = jnp.zeros((PACK_DEVS - 1,) + last.shape[1:], values.dtype)
    return jnp.concatenate([main, jnp.concatenate([last, none], axis=0)], axis=1)


def from_slots(slots):
    main = slots[:, : MAIN * HEAD_DIM].reshape(PACK_DEVS * MAIN * HEAD_DIM, -1)
    return jnp.concatenate([main, slots[0, MAIN * HEAD_DIM :]], axis=0)


def pack_exchange(value):
    count = lax.axis_size("fsdp")
    groups = [list(range(first, first + PACK_DEVS)) for first in range(0, count, PACK_DEVS)]
    return lax.all_to_all(value, "fsdp", 0, 0, axis_index_groups=groups)


def plane_first(quarter):
    return chip_swap(quarter, 1), chip_swap(quarter, 2)


def plane_second(got):
    return chip_swap(got[0][0], 2), chip_swap(got[1][1], 1)


def plane_whole(quarter, got, across):
    return tuple(jnp.concatenate([quarter[i], got[0][i], got[1][i], across[i]], axis=0) for i in range(2))


def sum_first(left, right):
    return chip_swap(left[3], 2), chip_swap(right[3], 1), chip_swap(left[2], 2), chip_swap(right[1], 1)


def sum_second(left, right, got):
    to_x = (left[1].astype(F32) + got[0].astype(F32)).astype(BF)
    to_y = (right[2].astype(F32) + got[1].astype(F32)).astype(BF)
    return chip_swap(to_x, 1), chip_swap(to_y, 2)


def sum_whole(left, right, got, last):
    left = left[0].astype(F32) + got[2].astype(F32) + last[0].astype(F32)
    right = right[0].astype(F32) + got[3].astype(F32) + last[1].astype(F32)
    return left.astype(BF), right.astype(BF)


def bits_of(count):
    return count.bit_length() - 1


def gather_bit(rows, bit):
    return ordered((lax.axis_index("fsdp") >> bit) & 1, rows, chip_swap(rows, 1 << bit), 0)


def reduce_vector(rows):
    index = lax.axis_index("fsdp")
    for bit in range(bits_of(lax.axis_size("fsdp"))):
        split = rows.reshape(-1, 2, rows.shape[-1])
        mine = (index >> bit) & 1
        rows = take(split, mine, 1, 1) + chip_swap(take(split, 1 - mine, 1, 1), 1 << bit)
        rows = rows[:, 0]
    return rows[0]


def on_device(
    inputs,
    cotangent,
    segments,
    ln1_gain,
    ln1_bias,
    w_qkv,
    b_qv,
    w_out,
    b_out,
    ln2_gain,
    ln2_bias,
    w_fc,
    b_fc,
    w_proj,
    b_proj,
):
    core = lax.axis_index("section")
    rank = lax.axis_index("fsdp")
    count = lax.axis_size("fsdp")
    bits = bits_of(count)
    tokens, width = inputs.shape[1:]
    shard = w_qkv.shape[1]
    hidden = w_fc.shape[2]
    quarter = width // 4
    pair_bit = (rank >> 2) & 1
    plane = rank & 3

    lines = count // 8

    place = jnp.arange(width, dtype=jnp.int32)
    block = place // shard
    line = block % (2 * lines)
    natural_line = ((((rank >> 3) ^ (line >> 1)) << 1) | (line & 1)) * 4 + ((place // quarter) ^ plane)
    natural_line = natural_line * shard + place % shard
    natural_side = (((block >> 3) * 2 + (block & 1)) * 4 + ((block >> 1) & 3)) * shard + place % shard

    def reorder(values, order):
        return dot(values, order).astype(BF)

    def reorder_back(values, order):
        return dot_cols(values, order).astype(BF)

    def reorder_wide(values, order):
        top = values.astype(BF)
        return dot(top, order) + dot((values - top.astype(F32)).astype(BF), order)

    qkv_half = 3 * width // 2
    out_half = width // 2
    small = hidden // 4
    planes = [list(range(first, first + 4)) for first in range(0, count, 4)]
    sides = [[i for i in range(count) if (i >> 2) & 1 == side] for side in range(2)]

    def by_side(piece):
        half = piece.shape[-1] // 2
        return take(piece, pair_bit, half, 2), take(piece, 1 - pair_bit, half, 2)

    def line_rows(same, other):
        rows = ordered(pair_bit, jnp.stack(same)[:, None], jnp.stack(other)[:, None], 1)
        return jnp.moveaxis(rows, 2, 0).reshape(2, quarter, -1)

    def line_first(mine, yours):
        same = [mine] + [chip_swap(mine, m << 3) for m in range(1, lines)]
        return same, [chip_swap(yours, (m << 3) | 4) for m in range(lines)]

    def gather_side(mine, got):
        rows = ordered(pair_bit, mine, got, 1)
        rows = jnp.concatenate([rows[0], rows[1]], axis=1)
        return lax.all_gather(rows, "fsdp", axis_index_groups=sides, tiled=True)

    def line_terms(rows, columns):
        return [dot_rows(rows[:, k * quarter : (k + 1) * quarter], columns).astype(BF) for k in range(4)]

    def owner_terms(rows, columns):
        return dot_rows(rows, columns).astype(BF).reshape(4, quarter, -1)

    def line_by_owner(rows):
        parts = [lax.dynamic_slice_in_dim(rows, (k ^ plane) * quarter, quarter, 1) for k in range(4)]
        return jnp.concatenate(parts, axis=1)

    def side_by_owner(rows):
        size = 2 * shard
        parts = [rows[:, (m * 4 + k) * size : (m * 4 + k + 1) * size] for k in range(4) for m in range(lines)]
        return jnp.concatenate(parts, axis=1)

    def plane_sum(terms):
        return lax.psum_scatter(terms, "fsdp", scatter_dimension=0, axis_index_groups=planes)

    def beside(left, right):
        return jnp.concatenate(
            [
                jnp.concatenate([left, jnp.zeros((left.shape[0], right.shape[1]), BF)], axis=1),
                jnp.concatenate([jnp.zeros((right.shape[0], left.shape[1]), BF), right], axis=1),
            ],
            axis=0,
        )

    def line_pieces(totals, relative):
        totals = [total.reshape(lines, 2, shard, -1) for total in totals]

        def pieces(index):
            rows = jnp.concatenate([take(total, index, 1, 1)[:, 0] for total in totals], axis=-1)
            if relative:
                return [rows[m] for m in range(lines)]
            return [lax.dynamic_index_in_dim(rows, (rank >> 3) ^ m, 0, False) for m in range(lines)]

        return pieces(pair_bit), pieces(1 - pair_bit)

    def line_sum_first(pieces):
        mine, yours = pieces
        same = [chip_swap(mine[m], m << 3) for m in range(1, lines)]
        other = [chip_swap(yours[m], (m << 3) | 4) for m in range(lines)]
        return same, other

    def line_sum_whole(pieces, got):
        same, other = got
        mine = pieces[0][0].astype(F32)
        for piece in same:
            mine = mine + piece.astype(F32)
        yours = other[0].astype(F32)
        for piece in other[1:]:
            yours = yours + piece.astype(F32)
        return mine, yours

    def halves(own, other):
        return ordered(core, own, other, 1)

    def gather_tokens(values):
        two = jnp.concatenate([values, chip_swap(values, 4)], axis=0)
        return jnp.concatenate([two, core_swap(two)], axis=0)

    def reduce_tokens(values):
        two = values[: 2 * tokens] + core_swap(values[2 * tokens :].astype(BF)).astype(F32)
        return two[:tokens] + chip_swap(two[tokens:].astype(BF), 4).astype(F32)

    def attn_in(layer, rows_line):
        normed_float, norm_back = jax.vjp(norm_rows, rows_line, *layer_vectors[layer][0])
        return normed_float.astype(BF), norm_back

    def attn_qkv(layer, normed, attn_own, attn_other):
        both = [jnp.concatenate([dot(normed, w) for w in part], axis=1)[:, :qkv_half] for part in (attn_own, attn_other)]
        packed = halves(*both) + layer_vectors[layer][2]
        packed = packed.astype(BF).T
        return jnp.concatenate([to_slots(packed[i * width : (i + 1) * width]) for i in range(3)], axis=1)

    def attn_mix(heads_packed):
        heads_ctx, probs = attend(heads_packed, pack_segments)
        return pack_exchange(heads_ctx), probs

    def attn_out(layer, rows_in, heads_ctx, attn_own, attn_other):
        out_bias, gain, bias, _ = layer_vectors[layer][1]
        context = reorder(from_slots(heads_ctx).T, order_line)
        both = [jnp.concatenate([dot(context, w) for w in part], axis=1)[:, qkv_half:] for part in (attn_own, attn_other)]
        middle = rows_in + reorder_wide(halves(*both), order_side) + out_bias
        normed_float, norm_back = jax.vjp(norm_rows, middle, gain, bias)
        return context, middle, normed_float.astype(BF), norm_back

    def mlp(layer, middle, normed, fc_weight, proj_weight):
        pre_act = dot(normed, fc_weight) + layer_vectors[layer][3]
        activated = gelu_tanh(pre_act).astype(BF)
        result = middle + reduce_tokens(dot_cols(activated, proj_weight)) + layer_vectors[layer][1][3]
        return result, pre_act, activated

    def mlp_back(grad_out_all, pre_act, fc_weight, proj_weight):
        grad_act = dot(grad_out_all, proj_weight)
        grad_pre = jax.vjp(gelu_tanh, pre_act)[1](grad_act)[0].astype(BF)
        return grad_pre, dot_cols(grad_pre, fc_weight)

    def back_through(grad, blocks, first, last):
        total, start = 0.0, 0
        for w in blocks:
            stop = start + w.shape[1]
            low, high = max(first, start), min(last, stop)
            if low < high:
                part = jnp.pad(grad[:, low - first : high - first], ((0, 0), (low - start, stop - high)))
                total += dot_cols(part, w)
            start = stop
        return total

    def attn_out_back(upstream, grad_norm, norm_back, attn_own, attn_other):
        grad_middle_norm, grad_gain, grad_bias = norm_back(grad_norm)
        grad_middle = upstream + grad_middle_norm
        grad_attn_own = grad_middle.astype(BF)
        grad_attn = reorder_back(grad_attn_own, order_side)
        attn_mine, attn_yours = take(grad_attn, core, out_half, 1), take(grad_attn, 1 - core, out_half, 1)
        columns = qkv_half, qkv_half + out_half
        grad_context = back_through(attn_mine, attn_own, *columns) + back_through(attn_yours, attn_other, *columns)
        (grad_context,) = fence(reorder_back(grad_context.astype(BF), order_line))
        heads_grad = pack_exchange(to_slots(grad_context.T))
        return reorder_wide(grad_middle, order_across), grad_attn_own, attn_mine, attn_yours, heads_grad, grad_gain, grad_bias

    def attn_qkv_back(back, grad_middle, norm_back, attn_own, attn_other):
        grad_packed = jnp.concatenate(
            [from_slots(back[:, i * SLOT_COLS : (i + 1) * SLOT_COLS]) for i in range(3)], axis=0
        ).T
        mine, yours = take(grad_packed, core, qkv_half, 1), take(grad_packed, 1 - core, qkv_half, 1)
        grad_normed = back_through(mine, attn_own, 0, qkv_half) + back_through(yours, attn_other, 0, qkv_half)
        grad_rows_norm, grad_gain, grad_bias = norm_back(grad_normed)
        return grad_middle + grad_rows_norm, grad_packed, mine, yours, grad_gain, grad_bias

    def attn_factors(normed, context, qkv_mine, qkv_yours, attn_mine, attn_yours):
        got = core_swap(jnp.concatenate([normed, context, qkv_yours, attn_yours], axis=1))
        normed_both = jnp.concatenate([normed, got[:, :width]], axis=0)
        context_both = jnp.concatenate([context, got[:, width : 2 * width]], axis=0)
        qkv_both = jnp.concatenate([qkv_mine, got[:, 2 * width : 2 * width + qkv_half]], axis=0)
        attn_both = jnp.concatenate([attn_mine, got[:, 2 * width + qkv_half :]], axis=0)
        return normed_both, context_both, qkv_both, attn_both

    def vector_grads(gain_one, bias_one, grad_attn_own, gain_two, bias_two, grad_out_low, grad_packed, grad_pre):
        def natural(rows, order):
            return lax.dot_general(
                jnp.stack(rows),
                order.astype(F32),
                (((1,), (1,)), ((), ())),
                precision=lax.Precision.HIGHEST,
                preferred_element_type=F32,
            )

        out_bias = jnp.sum(grad_attn_own.astype(F32), axis=0)
        proj_bias = jnp.sum(grad_out_low.astype(F32), axis=0)
        model = jnp.concatenate(
            [natural([gain_one, bias_one], order_line), natural([out_bias, gain_two, bias_two, proj_bias], order_side)]
        )
        packed_float = grad_packed.astype(F32)
        qv = jnp.concatenate([jnp.sum(packed_float[:, :width], axis=0), jnp.sum(packed_float[:, 2 * width :], axis=0)])
        fc = lax.dynamic_update_slice_in_dim(
            jnp.zeros((hidden,), F32),
            jnp.sum(grad_pre.astype(F32), axis=0),
            core * (hidden // 2) + pair_bit * small,
            0,
        )
        return jnp.concatenate(
            [model[i].reshape(count, shard) for i in range(6)]
            + [qv.reshape(count, 2 * shard), fc.reshape(count, 4 * shard)],
            axis=1,
        )

    def two(first, second):
        halves_of = []
        for index in (core, 1 - core):
            left, right = [take(p, index, p.shape[1] // 2, 1) for p in (first, second)]
            size = (left.shape[1] + right.shape[1]) // 2
            if left.shape[1] > size:
                left, right = left[:, :size], jnp.concatenate([left[:, size:], right], axis=1)
            halves_of.append(jnp.stack([left, right]))
        mine, yours = halves_of
        got = core_swap(yours)
        return [jnp.where(core == layer, mine, got) for layer in range(2)]

    attn_shards = two(w_qkv[0], w_out[0])
    vectors = jnp.concatenate(
        [
            ln1_gain[0],
            ln1_bias[0],
            b_out[0],
            ln2_gain[0],
            ln2_bias[0],
            b_proj[0],
            b_qv[0],
            b_fc[0],
            lax.dynamic_index_in_dim(segments, core, 0, False).astype(BF),
        ]
    )
    (a0, a1), vectors = fence(attn_shards, vectors)

    a0_line = line_first(a0, a0)
    mlp_shards = two(w_fc[0], w_proj[0])
    m0, m0_yours = by_side(mlp_shards[0])
    m1, m1_yours = by_side(mlp_shards[1])
    vector_rows = vectors[None]
    for bit in range(bits):
        vector_rows = gather_bit(vector_rows, bit)
    a0_line, a1, m0, m0_yours, m1, m1_yours, vector_rows = fence(
        a0_line, a1, m0, m0_yours, m1, m1_yours, vector_rows
    )

    a0_quarter = line_rows(*a0_line)
    a0_got = plane_first(a0_quarter)
    a1_line = line_first(a1, a1)
    m0_near = chip_swap(m0_yours, 4)
    own_inputs = lax.dynamic_index_in_dim(inputs, core, 0, False)
    own_cotangent = lax.dynamic_index_in_dim(cotangent, core, 0, False)
    order_line = (place[:, None] == natural_line[None, :]).astype(BF)
    order_side = (place[:, None] == natural_side[None, :]).astype(BF)
    order_across = (natural_side[:, None] == natural_line[None, :]).astype(BF)
    a0_quarter, a0_got, a1_line, m0_near, order_line, order_side, order_across, vector_rows, own_cotangent = fence(
        a0_quarter, a0_got, a1_line, m0_near, order_line, order_side, order_across, vector_rows, own_cotangent
    )

    a0_across = plane_second(a0_got)
    a0_quarter_other, a0_got_other = core_swap(a0_quarter), (core_swap(a0_got[0]), core_swap(a0_got[1]))
    a1_quarter = line_rows(*a1_line)
    a1_got = plane_first(a1_quarter)
    segment_rows = vector_rows[:, 12 * shard :].astype(jnp.int32)
    pack_segments = take(segment_rows, rank // PACK_DEVS, PACK_DEVS, 0).reshape(-1)
    vector_rows = vector_rows[:, : 12 * shard]
    vector_other = core_swap(vector_rows)
    layer_vectors = []
    for layer in range(2):
        rows = jnp.where(core == layer, vector_rows, vector_other)
        model = jnp.stack([rows[:, i * shard : (i + 1) * shard].reshape(width) for i in range(6)])
        norm_one, rest = dot(model[:2], order_line), dot(model[2:], order_side)
        qv = rows[:, 6 * shard : 8 * shard].reshape(2 * width).astype(F32)
        fc = rows[:, 8 * shard : 12 * shard].reshape(hidden).astype(F32)
        fc = lax.dynamic_slice_in_dim(fc, core * (hidden // 2) + pair_bit * (hidden // 4), hidden // 4, 0)
        qkv = jnp.concatenate([qv[:width], jnp.zeros((width,), F32), qv[width:]])
        layer_vectors.append(((norm_one[0], norm_one[1]), (rest[0], rest[1], rest[2], rest[3]), qkv, fc))
    first_in = reorder(own_inputs, order_side).astype(F32)
    first_line = reorder(own_inputs, order_line).astype(F32)
    first_normed, first_norm_one = attn_in(0, first_line)
    second_up_low = reorder(own_cotangent, order_side)
    second_up_all = gather_tokens(second_up_low)
    (
        a0_across,
        a0_quarter_other,
        a0_got_other,
        a1_quarter,
        a1_got,
        first_normed,
        second_up_low,
        second_up_all,
        m0,
        m0_near,
        m1_yours,
    ) = fence(
        a0_across,
        a0_quarter_other,
        a0_got_other,
        a1_quarter,
        a1_got,
        first_normed,
        second_up_low,
        second_up_all,
        m0,
        m0_near,
        m1_yours,
    )

    mlp_first = gather_side(m0, m0_near)
    a1_across = plane_second(a1_got)
    a0_across_other = [core_swap(part) for part in a0_across]
    attn_first = (
        plane_whole(a0_quarter, a0_got, a0_across),
        plane_whole(a0_quarter_other, a0_got_other, a0_across_other),
    )
    sent = attn_qkv(0, first_normed, *attn_first)
    sent, a1_across, m1_yours = fence(sent, a1_across, m1_yours)

    m1_near = chip_swap(m1_yours, 4)
    first_heads = pack_exchange(sent)
    first_ctx, first_probs = attn_mix(first_heads)
    attn_second = plane_whole(a1_quarter, a1_got, a1_across)
    attn_second = attn_second, tuple(core_swap(part) for part in attn_second)
    first_context, first_middle, first_normed_two, first_norm_two = attn_out(0, first_in, first_ctx, *attn_first)
    first_normed_two, mlp_first, m1, m1_near = fence(first_normed_two, mlp_first, m1, m1_near)
    mlp_second = gather_side(m1, m1_near)
    first_normed_two = gather_tokens(first_normed_two)
    mlp_first = mlp_first[:, :small], mlp_first[:, small:]
    first_out, first_pre, first_act = mlp(0, first_middle, first_normed_two, *mlp_first)
    first_low = first_out.astype(BF)
    second_in = first_low.astype(F32)
    second_line = reorder(first_low, order_across).astype(F32)
    second_normed, second_norm_one = attn_in(1, second_line)
    second_heads = pack_exchange(attn_qkv(1, second_normed, *attn_second))
    second_ctx, second_probs = attn_mix(second_heads)
    second_ctx, mlp_second = fence(second_ctx, mlp_second)
    second_context, second_middle, second_normed_two, second_norm_two = attn_out(1, second_in, second_ctx, *attn_second)
    second_normed_two = gather_tokens(second_normed_two)
    mlp_second = mlp_second[:, :small], mlp_second[:, small:]
    second_out, second_pre, second_act = mlp(1, second_middle, second_normed_two, *mlp_second)
    second_low = second_out.astype(BF)

    second_up = second_up_low.astype(F32)
    second_pre_grad, part = mlp_back(second_up_all, second_pre, *mlp_second)
    second_pre_grad, part = fence(second_pre_grad, part)
    grad_norm = reduce_tokens(part)
    f1_terms = owner_terms(side_by_owner(second_normed_two), second_pre_grad)
    p1_terms = owner_terms(side_by_owner(second_up_all), second_act)
    grad_norm, f1_terms, p1_terms = fence(grad_norm, f1_terms, p1_terms)
    f1_sum, p1_sum = plane_sum(f1_terms), plane_sum(p1_terms)
    second_mid_grad, second_da, attn_mine, attn_yours, heads_grad, second_gain_two, second_bias_two = attn_out_back(
        second_up, grad_norm, second_norm_two, *attn_second
    )
    back = pack_exchange(attend_back(second_heads, second_probs, heads_grad))
    second_grad, second_packed, qkv_mine, qkv_yours, second_gain_one, second_bias_one = attn_qkv_back(
        back, second_mid_grad, second_norm_one, *attn_second
    )
    second_grad_low = second_grad.astype(BF)
    first_up_low = reorder_back(second_grad_low, order_across)
    first_up_low, qkv_mine, qkv_yours = fence(first_up_low, qkv_mine, qkv_yours)
    first_up = first_up_low.astype(F32)
    first_up_all = gather_tokens(first_up_low)
    normed_both, context_both, qkv_both, attn_both = attn_factors(
        second_normed, second_context, qkv_mine, qkv_yours, attn_mine, attn_yours
    )
    q1_terms = owner_terms(line_by_owner(normed_both), qkv_both)
    o1_terms = owner_terms(line_by_owner(context_both), attn_both)
    first_up_all, q1_terms, o1_terms, f1_sum = fence(first_up_all, q1_terms, o1_terms, f1_sum)
    q1_sum, o1_sum = plane_sum(q1_terms), plane_sum(o1_terms)
    first_pre_grad, part = mlp_back(first_up_all, first_pre, *mlp_first)
    first_pre_grad, part = fence(first_pre_grad, part)
    grad_norm = reduce_tokens(part)
    f0_terms = owner_terms(side_by_owner(first_normed_two), first_pre_grad)
    p0_terms = owner_terms(side_by_owner(first_up_all), first_act)
    grad_norm, f0_terms, p0_terms, p1_sum = fence(grad_norm, f0_terms, p0_terms, p1_sum)
    f0_sum, p0_sum = plane_sum(f0_terms), plane_sum(p0_terms)
    m1_pieces = line_pieces((f1_sum, p1_sum), False)
    m1_got = line_sum_first(m1_pieces)
    first_mid_grad, first_da, attn_mine, attn_yours, heads_grad, first_gain_two, first_bias_two = attn_out_back(
        first_up, grad_norm, first_norm_two, *attn_first
    )
    heads_grad, first_mid_grad, m1_got, attn_mine, attn_yours, q1_sum = fence(
        heads_grad, first_mid_grad, m1_got, attn_mine, attn_yours, q1_sum
    )
    def by_section(first, second):
        own = jnp.where(core == 0, first, second)
        got = core_swap(jnp.where(core == 0, second, first))
        return ordered(core, own[None], got[None], 0)

    back = pack_exchange(attend_back(first_heads, first_probs, heads_grad))
    section_outputs = by_section(reorder_back(first_low, order_side), reorder_back(second_low, order_side))
    second_vectors = vector_grads(
        second_gain_one,
        second_bias_one,
        second_da,
        second_gain_two,
        second_bias_two,
        second_up_low,
        second_packed,
        second_pre_grad,
    )
    back, o1_sum, section_outputs, second_vectors = fence(back, o1_sum, section_outputs, second_vectors)
    a1_pieces = line_pieces((q1_sum, o1_sum), True)
    a1_got = line_sum_first(a1_pieces)
    first_grad, first_packed, qkv_mine, qkv_yours, first_gain_one, first_bias_one = attn_qkv_back(
        back, first_mid_grad, first_norm_one, *attn_first
    )
    first_grad_low = first_grad.astype(BF)
    normed_both, context_both, qkv_both, attn_both = attn_factors(
        first_normed, first_context, qkv_mine, qkv_yours, attn_mine, attn_yours
    )
    a0_left = line_terms(normed_both, qkv_both[:, :width])
    a0_right = line_terms(
        jnp.concatenate([normed_both, context_both], axis=0), beside(qkv_both[:, width:], attn_both)
    )
    a0_left, a0_right, first_grad_low = fence(a0_left, a0_right, first_grad_low)
    a0_got = sum_first(a0_left, a0_right)
    a0_got, a1_got, f0_sum, p0_sum, first_grad_low, first_packed = fence(
        a0_got, a1_got, f0_sum, p0_sum, first_grad_low, first_packed
    )
    first_vectors = vector_grads(
        first_gain_one,
        first_bias_one,
        first_da,
        first_gain_two,
        first_bias_two,
        first_up_low,
        first_packed,
        first_pre_grad,
    )
    vector_rows = jnp.where(core == 0, first_vectors, second_vectors) + core_swap(
        jnp.where(core == 0, second_vectors, first_vectors)
    )
    a0_last = sum_second(a0_left, a0_right, a0_got)
    m0_pieces = line_pieces((f0_sum, p0_sum), False)
    m0_got = line_sum_first(m0_pieces)
    input_grads = by_section(
        reorder_back(first_grad_low, order_line), reorder_back(second_grad_low, order_line)
    )
    a0_last, m0_got, input_grads, vector_rows = fence(a0_last, m0_got, input_grads, vector_rows)
    vector_own = reduce_vector(vector_rows)
    a0_pieces = line_pieces(sum_whole(a0_left, a0_right, a0_got, a0_last), True)
    a0_got = line_sum_first(a0_pieces)

    def matrix_grads(attn_pieces, attn_got, mlp_pieces, mlp_got):
        same, other = line_sum_whole(attn_pieces, attn_got)
        attn = same + other
        same, other = line_sum_whole(mlp_pieces, mlp_got)
        return (
            attn[:, :qkv_half],
            attn[:, qkv_half:],
            ordered(pair_bit, same[:, :small], other[:, :small], 1),
            ordered(pair_bit, same[:, small:], other[:, small:], 1),
        )

    first_mats = matrix_grads(a0_pieces, a0_got, m0_pieces, m0_got)
    second_mats = matrix_grads(a1_pieces, a1_got, m1_pieces, m1_got)
    mats = []
    for first, second in zip(first_mats, second_mats):
        own = jnp.where(core == 0, first, second)
        got = core_swap(jnp.where(core == 0, second, first))
        mats.append(ordered(core, own, got, 1))
    model = [vector_own[i * shard : (i + 1) * shard] for i in range(6)]
    return (
        section_outputs[None],
        input_grads[None],
        model[0][None],
        model[1][None],
        mats[0][None],
        vector_own[6 * shard : 8 * shard][None],
        mats[1][None],
        model[2][None],
        model[3][None],
        model[4][None],
        mats[2][None],
        vector_own[8 * shard :][None],
        mats[3][None],
        model[5][None],
    )


def solution(mesh):
    in_specs = (
        P(None, "fsdp", None),
        P(None, "fsdp", None),
        P(None, "fsdp"),
        P("section", "fsdp"),
        P("section", "fsdp"),
        P("section", "fsdp", None),
        P("section", "fsdp"),
        P("section", "fsdp", None),
        P("section", "fsdp"),
        P("section", "fsdp"),
        P("section", "fsdp"),
        P("section", "fsdp", None),
        P("section", "fsdp"),
        P("section", "fsdp", None),
        P("section", "fsdp"),
    )
    out_specs = (
        P("section", None, "fsdp", None),
        P("section", None, "fsdp", None),
        P("section", "fsdp"),
        P("section", "fsdp"),
        P("section", "fsdp", None),
        P("section", "fsdp"),
        P("section", "fsdp", None),
        P("section", "fsdp"),
        P("section", "fsdp"),
        P("section", "fsdp"),
        P("section", "fsdp", None),
        P("section", "fsdp"),
        P("section", "fsdp", None),
        P("section", "fsdp"),
    )
    return jax.shard_map(
        on_device, mesh=mesh, in_specs=in_specs, out_specs=out_specs, check_vma=False
    )
```

time: 1450 us -> 1380 us (0.952)
  waiting for transfers between devices: 601 us -> 508 us
  matrix products: 224 us -> 314 us
  other arithmetic: 187 us -> 136 us
  local copies, waits for them, and re-layouts: 200 us -> 177 us
  starting transfers between devices: 171 us -> 150 us
    ppermute x64 -> x50, waiting for transfers between devices: 558 us -> 392 us  [chip_swap(): return lax.ppermute(value, 'fsdp', [(i, i ^ mask) for i in range(count)])]
    dot_general x22 -> x34, matrix products: 92.2 us -> 140 us  [dot(): return jnp.dot(left, right, preferred_element_type=F32)]
    squeeze x4 -> x22, local copies, waits for them, and re-layouts: 0.9 us -> 43.7 us  [the longest x8 17.1 us: pieces(): take(total, index, 1, 1)[:, 0]]
    concatenate x26 -> x19, other arithmetic: 67.8 us -> 30.4 us  [the longest x2 23.2 us: plane_whole(): jnp.concatenate([quarter[i], got[0][i], got[1][i], across[i]], axis=0)]
    dot_general x18 -> x23, matrix products: 67.9 us -> 104 us  [dot_cols(): lax.dot_general(left, right, (((1,), (1,)), ((), ())), preferred_element_...]
    all_to_all x8 -> x7, waiting for transfers between devices: 42.3 us -> 76.3 us  [pack_exchange(): return lax.all_to_all(value, 'fsdp', 0, 0, axis_index_groups=groups)]
    unnamed x0 -> x14, waiting for transfers between devices: none -> 32.6 us
    all_to_all x8 -> x7, starting transfers between devices: 60.1 us -> 31.9 us  [pack_exchange(): return lax.all_to_all(value, 'fsdp', 0, 0, axis_index_groups=groups)]
  transfers between devices with their start and end apart: 100 -> 92, of which waited for: 31 -> 43; matrix products, arithmetic and copies ran while one was open for 41% -> 38% of each run, Pallas kernels for 3% -> 4%
where the time goes in v2:
time: 1380 us; the launch traced here: 1370 us
  waiting for transfers between devices  508 us (37%)
  matrix products  314 us (23%)
  local copies, waits for them, and re-layouts  177 us (13%)
  starting transfers between devices  150 us (11%)
  other arithmetic  136 us (10%)
  Pallas kernels  49.6 us (4%)
  between operations  18.9 us (1%)
  blocking collectives  14.1 us (1%)
    ppermute x50, waiting for transfers between devices, chip_swap(): return lax.ppermute(value, 'fsdp', [(i, i ^ mask) for i in range(count)])  392 us
    dot_general x34, matrix products, dot(): return jnp.dot(left, right, preferred_element_type=F32)  140 us
    ppermute x50, starting transfers between devices, chip_swap(): return lax.ppermute(value, 'fsdp', [(i, i ^ mask) for i in range(count)])  113 us
    dot_general x23, matrix products, dot_cols(): lax.dot_general(left, right, (((1,), (1,)), ((), ())), preferred_element_...  104 us
    all_to_all x7, waiting for transfers between devices, pack_exchange(): return lax.all_to_all(value, 'fsdp', 0, 0, axis_index_groups=groups)  76.3 us
    unnamed x491, local copies, waits for them, and re-layouts  47.8 us
    dot_general x14, matrix products, dot_rows(): lax.dot_general(left, right, (((0,), (0,)), ((), ())), preferred_element_...  44.6 us
    unnamed x14, waiting for transfers between devices  32.6 us
  transfers between devices with their start and end apart: 92, of which 43 were waited for; matrix products, arithmetic and copies ran while one was open for 38% of the time, Pallas kernels for 4%

profile of v2, /device:TPU:0, one launch (start us, length us, event | category | flops | bytes accessed | tf_op | source)
XLA Modules:
  0.0 1366.6 jit_solution(12940723912396202485)
XLA Ops:
  66.5 26.4 %collective-permute-done.1 = bf16[2,100,1600]{2,0,1:T(2,128)(2,1)S(1)} collective-permute-done((bf16[2,100,1600]{2,0,1:T(2,128)(2,1)S(1)}, bf16[2,100,1600]{2,0,1:T(2,128)(2,1)S(1)}, u32[]{:S(2)}, u32[]{:S(2)}) %collective-permute-start.1) | collective-permute-done | bytes 640032 | tf_op jit(solution)/shard_map/ppermute | solution.py:24
  109.5 15.4 %collective-permute-done.13 = bf16[2,100,1600]{2,0,1:T(2,128)(2,1)S(1)} collective-permute-done((bf16[2,100,1600]{2,0,1:T(2,128)(2,1)}, bf16[2,100,1600]{2,0,1:T(2,128)(2,1)S(1)}, u32[]{:S(2)}, u32[]{:S(2)}) %collective-permute-start.13) | collective-permute-done | bytes 640032 | tf_op jit(solution)/shard_map/ppermute | solution.py:24
  124.9 12.4 collective-permute-start.14
  145.9 15.2 %collective-permute-done.11 = bf16[2,100,1600]{2,0,1:T(2,128)(2,1)S(1)} collective-permute-done((bf16[2,100,1600]{2,0,1:T(2,128)(2,1)}, bf16[2,100,1600]{2,0,1:T(2,128)(2,1)S(1)}, u32[]{:S(2)}, u32[]{:S(2)}) %collective-permute-start.11) | collective-permute-done | bytes 640032 | tf_op jit(solution)/shard_map/ppermute | solution.py:24
  188.4 15.5 %collective-permute-done.15 = bf16[400,1600]{1,0:T(8,128)(2,1)} collective-permute-done((bf16[400,1600]{1,0:T(8,128)(2,1)}, bf16[400,1600]{1,0:T(8,128)(2,1)}, u32[]{:S(2)}, u32[]{:S(2)}) %collective-permute-start.15) | collective-permute-done | bytes 1280032 | tf_op jit(solution)/shard_map/ppermute | solution.py:24
  219.7 38.8 %collective-permute-done.21 = bf16[2,400,1600]{2,1,0:T(8,128)(2,1)} collective-permute-done((bf16[2,400,1600]{2,1,0:T(8,128)(2,1)}, bf16[2,400,1600]{2,1,0:T(8,128)(2,1)}, u32[]{:S(2)}, u32[]{:S(2)}) %collective-permute-start.21) | collective-permute-done | bytes 2560032 | tf_op jit(solution)/shard_map/ppermute | solution.py:24
  301.4 21.2 %collective-permute-done.27 = bf16[400,1600]{1,0:T(8,128)(2,1)S(1)} collective-permute-done((bf16[400,1600]{1,0:T(8,128)(2,1)S(1)}, bf16[400,1600]{1,0:T(8,128)(2,1)S(1)}, u32[]{:S(2)}, u32[]{:S(2)}) %collective-permute-start.27) | collective-permute-done | bytes 1280032 | tf_op jit(solution)/shard_map/ppermute | solution.py:24
  327.9 28.1 %all-to-all-done.q_ref.k_ref.v_ref = bf16[8,768,128]{2,1,0:T(8,128)(2,1)S(1)} async-done(((bf16[8,768,128]{2,1,0:T(8,128)(2,1)}), bf16[8,768,128]{2,1,0:T(8,128)(2,1)S(1)}, u32[]{:S(2)}, u32[]{:S(2)}) %all-to-all-start) | async-done | bytes 1572896 | tf_op jit(solution)/shard_map/all_to_all | solution.py:211
  356.0 12.4 shard_map.254
  403.3 27.7 %collective-permute-done.29 = bf16[2,100,1600]{2,1,0:T(8,128)(2,1)} collective-permute-done((bf16[2,100,1600]{2,1,0:T(8,128)(2,1)}, bf16[2,100,1600]{2,1,0:T(8,128)(2,1)}, u32[]{:S(2)}, u32[]{:S(2)}) %collective-permute-start.29) | collective-permute-done | bytes 640032 | tf_op jit(solution)/shard_map/ppermute | solution.py:24
  438.3 11.6 pad_maximum_fusion.5
  452.3 11.6 pad_maximum_fusion.4
  487.4 23.7 %collective-permute-done.33 = bf16[128,1600]{0,1:T(8,128)(2,1)S(1)} collective-permute-done((bf16[128,1600]{0,1:T(8,128)(2,1)S(1)}, bf16[128,1600]{0,1:T(8,128)(2,1)S(1)}, u32[]{:S(2)}, u32[]{:S(2)}) %collective-permute-start.33) | collective-permute-done | bytes 409632 | tf_op jit(solution)/shard_map/ppermute | solution.py:24
  543.6 25.0 %all-to-all-done.2.q_ref.k_ref.v_ref = bf16[8,768,128]{2,1,0:T(8,128)(2,1)} async-done(((bf16[8,768,128]{2,1,0:T(8,128)(2,1)}), bf16[8,768,128]{2,1,0:T(8,128)(2,1)}, u32[]{:S(2)}, u32[]{:S(2)}) %all-to-all-start.2) | async-done | bytes 1572896 | tf_op jit(solution)/shard_map/all_to_all | solution.py:211
  568.6 13.4 shard_map.255
  686.9 14.1 %all_to_all.40.d_ref = bf16[8,256,128]{2,1,0:T(8,128)(2,1)S(1)} all-to-all(bf16[8,256,128]{2,1,0:T(8,128)(2,1)S(1)} %fusion.150), channel_id=1, replica_groups={{0,1,2,3,4,5,6,7},{8,9,10,11,12,13,14,15},{16,17,18,19,20,21,22,23},{24..., dimensions={0} | all-to-all | bytes 1048576 | tf_op jit(solution)/shard_map/all_to_all | solution.py:211
  701.0 11.7 shard_map.256
  725.3 18.4 %all-to-all-done.5 = bf16[8,768,128]{2,1,0:T(8,128)(2,1)} async-done(((bf16[8,768,128]{2,1,0:T(8,128)(2,1)}), bf16[8,768,128]{2,1,0:T(8,128)(2,1)}, u32[]{:S(2)}, u32[]{:S(2)}) %all-to-all-start.5) | async-done | bytes 1572896 | tf_op jit(solution)/shard_map/all_to_all | solution.py:211
  914.4 19.2 %collective-permute-start.45 = (bf16[100,3200]{1,0:T(8,128)(2,1)}, bf16[100,3200]{1,0:T(8,128)(2,1)}, u32[]{:S(2)}, u32[]{:S(2)}) collective-permute-start(bf16[100,3200]{1,0:T(8,128)(2,1)} %fusion.145), channel_id=1, source_target_pairs={{0,8},{1,9},{2,10},{3,11},{4,12},{5,13},{6,14},{7,15},{8,0},{9,1},... | collective-permute-start | bytes 1920008 | tf_op jit(solution)/shard_map/ppermute | solution.py:24
  997.7 12.1 shard_map.257
  1115.8 32.0 %reduce-scatter.29.cloned.1.call-done = bf16[1,400,1600]{2,1,0:T(8,128)(2,1)} async-done(((bf16[4,400,1600]{2,1,0:T(8,128)(2,1)}), bf16[1,400,1600]{2,1,0:T(8,128)(2,1)}) %reduce-scatter.29.cloned.1.call-update) | async-done | bytes 1280016
  1147.8 21.3 %collective-permute-done.54 = bf16[400,1600]{1,0:T(8,128)(2,1)} collective-permute-done((bf16[400,1600]{1,0:T(8,128)(2,1)}, bf16[400,1600]{1,0:T(8,128)(2,1)}, u32[]{:S(2)}, u32[]{:S(2)}) %collective-permute-start.54) | collective-permute-done | bytes 1280032 | tf_op jit(solution)/shard_map/ppermute | solution.py:24
  1203.9 35.9 %collective-permute-done.61 = bf16[100,3200]{1,0:T(8,128)(2,1)} collective-permute-done((bf16[100,3200]{1,0:T(8,128)(2,1)}, bf16[100,3200]{1,0:T(8,128)(2,1)}, u32[]{:S(2)}, u32[]{:S(2)}) %collective-permute-start.61) | collective-permute-done | bytes 640032 | tf_op jit(solution)/shard_map/ppermute | solution.py:24
  1290.5 33.5 %collective-permute-done.68 = f32[2,1,1200]{2,1,0:T(1,128)S(1)} collective-permute-done((f32[2,1,1200]{2,1,0:T(1,128)S(1)}, f32[2,1,1200]{2,1,0:T(1,128)S(1)}, u32[]{:S(2)}, u32[]{:S(2)}) %collective-permute-start.68) | collective-permute-done | bytes 9632 | tf_op jit(solution)/shard_map/ppermute | solution.py:24
  (1075 shorter events, 851.1 us)
Async XLA Ops:
  7.2 423.7 %all-gather.3.cloned.1.call-start = ((), (), s32[]{:S(2)}) async-start(), calls=%async_computation.14 | async-start | bytes 11520000 | tf_op jit(solution)/shard_map/all_gather | solution.py:328
  100.6 64.0 %collective-permute-start.10 = (bf16[2,400,1600]{2,1,0:T(8,128)(2,1)}, bf16[2,400,1600]{2,1,0:T(8,128)(2,1)}, u32[]{:S(2)}, u32[]{:S(2)}) collective-permute-start(bf16[2,400,1600]{2,1,0:T(8,128)(2,1)} %reshape.859), channel_id=1, source_target_pairs={{0,2},{1,3},{2,0},{3,1},{4,6},{5,7},{6,4},{7,5},{8,10},{9,11},{10,... | collective-permute-start | bytes 7680008 | tf_op jit(solution)/shard_map/ppermute | solution.py:24
  102.2 62.4 %collective-permute-start.9 = (bf16[2,400,1600]{2,1,0:T(8,128)(2,1)}, bf16[2,400,1600]{2,1,0:T(8,128)(2,1)}, u32[]{:S(2)}, u32[]{:S(2)}) collective-permute-start(bf16[2,400,1600]{2,1,0:T(8,128)(2,1)} %reshape.859), channel_id=1, source_target_pairs={{0,1},{1,0},{2,3},{3,2},{4,5},{5,4},{6,7},{7,6},{8,9},{9,8},{10,11... | collective-permute-start | bytes 7680008 | tf_op jit(solution)/shard_map/ppermute | solution.py:24
  186.6 71.9 %collective-permute-start.21 = (bf16[2,400,1600]{2,1,0:T(8,128)(2,1)}, bf16[2,400,1600]{2,1,0:T(8,128)(2,1)}, u32[]{:S(2)}, u32[]{:S(2)}) collective-permute-start(bf16[2,400,1600]{2,1,0:T(8,128)(2,1)} %reshape.860), channel_id=1, source_target_pairs={{0,2},{1,3},{2,0},{3,1},{4,6},{5,7},{6,4},{7,5},{8,10},{9,11},{10,... | collective-permute-start | bytes 7680008 | tf_op jit(solution)/shard_map/ppermute | solution.py:24
  187.2 75.0 %collective-permute-start.20 = (bf16[2,400,1600]{2,1,0:T(8,128)(2,1)}, bf16[2,400,1600]{2,1,0:T(8,128)(2,1)}, u32[]{:S(2)}, u32[]{:S(2)}) collective-permute-start(bf16[2,400,1600]{2,1,0:T(8,128)(2,1)} %reshape.860), channel_id=1, source_target_pairs={{0,1},{1,0},{2,3},{3,2},{4,5},{5,4},{6,7},{7,6},{8,9},{9,8},{10,11... | collective-permute-start | bytes 7680008 | tf_op jit(solution)/shard_map/ppermute | solution.py:24
  188.4 73.8 %collective-permute-start.18 = (bf16[2,400,1600]{2,1,0:T(8,128)(2,1)}, bf16[2,400,1600]{2,1,0:T(8,128)(2,1)}, u32[]{:S(2)}, u32[]{:S(2)}) collective-permute-start(bf16[2,400,1600]{2,1,0:T(8,128)(2,1)} %collective-permute-done.9), channel_id=1, source_target_pairs={{0,16},{16,0},{1,17},{17,1},{2,18},{18,2},{3,19},{19,3},{4,20},{20... | collective-permute-start | bytes 7680008 | tf_op jit(solution)/shard_map/ppermute | solution.py:28
  372.1 225.5 %all-gather.5.cloned.1.call-start = ((), (), s32[]{:S(2)}) async-start(), calls=%async_computation.15 | async-start | bytes 11520000 | tf_op jit(solution)/shard_map/all_gather | solution.py:328
  449.9 64.5 %collective-permute-start.35 = (bf16[1600,1600]{1,0:T(8,128)(2,1)}, bf16[1600,1600]{1,0:T(8,128)(2,1)}, u32[]{:S(2)}, u32[]{:S(2)}) collective-permute-start(bf16[1600,1600]{1,0:T(8,128)(2,1)} %pad_maximum_fusion.5), channel_id=1, source_target_pairs={{0,16},{16,0},{1,17},{17,1},{2,18},{18,2},{3,19},{19,3},{4,20},{20... | collective-permute-start | bytes 15360008 | tf_op jit(solution)/shard_map/ppermute | solution.py:28
  587.7 217.2 %reduce-scatter.19.cloned.1.call-start = ((), (), s32[]{:S(2)}) async-start(), calls=%async_computation.16 | async-start | bytes 6656000
  718.2 174.8 %reduce-scatter.21.cloned.1.call-start = ((), (), s32[]{:S(2)}) async-start(), calls=%async_computation.17 | async-start | bytes 6656000
  718.8 278.9 %reduce-scatter.23.cloned.1.call-start = ((), (), s32[]{:S(2)}) async-start(), calls=%async_computation.18 | async-start | bytes 9728000
  805.0 230.8 %reduce-scatter.25.cloned.1.call-start = ((), (), s32[]{:S(2)}) async-start(), calls=%async_computation.19 | async-start | bytes 3584000
  856.2 259.6 %reduce-scatter.27.cloned.1.call-start = ((), (), s32[]{:S(2)}) async-start(), calls=%async_computation.20 | async-start | bytes 6656000
  914.4 61.9 %collective-permute-start.45 = (bf16[100,3200]{1,0:T(8,128)(2,1)}, bf16[100,3200]{1,0:T(8,128)(2,1)}, u32[]{:S(2)}, u32[]{:S(2)}) collective-permute-start(bf16[100,3200]{1,0:T(8,128)(2,1)} %fusion.145), channel_id=1, source_target_pairs={{0,8},{1,9},{2,10},{3,11},{4,12},{5,13},{6,14},{7,15},{8,0},{9,1},... | collective-permute-start | bytes 1920008 | tf_op jit(solution)/shard_map/ppermute | solution.py:24
  1015.3 132.5 %reduce-scatter.29.cloned.1.call-start = ((), (), s32[]{:S(2)}) async-start(), calls=%async_computation.21 | async-start | bytes 6656000
  1086.3 61.5 %collective-permute-start.52 = (bf16[400,1600]{1,0:T(8,128)(2,1)}, bf16[400,1600]{1,0:T(8,128)(2,1)}, u32[]{:S(2)}, u32[]{:S(2)}) collective-permute-start(bf16[400,1600]{1,0:T(8,128)(2,1)} %convolution_convert_fusion.10), channel_id=1, source_target_pairs={{0,2},{1,3},{2,0},{3,1},{4,6},{5,7},{6,4},{7,5},{8,10},{9,11},{10,... | collective-permute-start | bytes 3840008 | tf_op jit(solution)/shard_map/ppermute | solution.py:24
  1087.9 59.9 %collective-permute-start.53 = (bf16[400,1600]{1,0:T(8,128)(2,1)}, bf16[400,1600]{1,0:T(8,128)(2,1)}, u32[]{:S(2)}, u32[]{:S(2)}) collective-permute-start(bf16[400,1600]{1,0:T(8,128)(2,1)} %convolution_convert_fusion.6), channel_id=1, source_target_pairs={{0,1},{1,0},{2,3},{3,2},{4,5},{5,4},{6,7},{7,6},{8,9},{9,8},{10,11... | collective-permute-start | bytes 3840008 | tf_op jit(solution)/shard_map/ppermute | solution.py:24
  1089.4 79.7 %collective-permute-start.54 = (bf16[400,1600]{1,0:T(8,128)(2,1)}, bf16[400,1600]{1,0:T(8,128)(2,1)}, u32[]{:S(2)}, u32[]{:S(2)}) collective-permute-start(bf16[400,1600]{1,0:T(8,128)(2,1)} %convolution_convert_fusion.11), channel_id=1, source_target_pairs={{0,2},{1,3},{2,0},{3,1},{4,6},{5,7},{6,4},{7,5},{8,10},{9,11},{10,... | collective-permute-start | bytes 3840008 | tf_op jit(solution)/shard_map/ppermute | solution.py:24
  1094.4 74.7 %collective-permute-start.55 = (bf16[400,1600]{1,0:T(8,128)(2,1)}, bf16[400,1600]{1,0:T(8,128)(2,1)}, u32[]{:S(2)}, u32[]{:S(2)}) collective-permute-start(bf16[400,1600]{1,0:T(8,128)(2,1)} %convolution_convert_fusion.8), channel_id=1, source_target_pairs={{0,1},{1,0},{2,3},{3,2},{4,5},{5,4},{6,7},{7,6},{8,9},{9,8},{10,11... | collective-permute-start | bytes 3840008 | tf_op jit(solution)/shard_map/ppermute | solution.py:24
  1177.1 68.1 %collective-permute-start.60 = (bf16[400,1600]{1,0:T(8,128)(2,1)}, bf16[400,1600]{1,0:T(8,128)(2,1)}, u32[]{:S(2)}, u32[]{:S(2)}) collective-permute-start(bf16[400,1600]{1,0:T(8,128)(2,1)} %add_convert_fusion.2), channel_id=1, source_target_pairs={{0,2},{1,3},{2,0},{3,1},{4,6},{5,7},{6,4},{7,5},{8,10},{9,11},{10,... | collective-permute-start | bytes 3840008 | tf_op jit(solution)/shard_map/ppermute | solution.py:24
  1181.3 63.9 %collective-permute-start.59 = (bf16[400,1600]{1,0:T(8,128)(2,1)}, bf16[400,1600]{1,0:T(8,128)(2,1)}, u32[]{:S(2)}, u32[]{:S(2)}) collective-permute-start(bf16[400,1600]{1,0:T(8,128)(2,1)} %add_convert_fusion.3), channel_id=1, source_target_pairs={{0,1},{1,0},{2,3},{3,2},{4,5},{5,4},{6,7},{7,6},{8,9},{9,8},{10,11... | collective-permute-start | bytes 3840008 | tf_op jit(solution)/shard_map/ppermute | solution.py:24
  1267.1 70.4 %collective-permute-start.70 = (bf16[100,3200]{1,0:T(8,128)(2,1)}, bf16[100,3200]{1,0:T(8,128)(2,1)}, u32[]{:S(2)}, u32[]{:S(2)}) collective-permute-start(bf16[100,3200]{1,0:T(8,128)(2,1)} %fusion.148), channel_id=1, source_target_pairs={{0,8},{1,9},{2,10},{3,11},{4,12},{5,13},{6,14},{7,15},{8,0},{9,1},... | collective-permute-start | bytes 1920008 | tf_op jit(solution)/shard_map/ppermute | solution.py:24
  1279.0 58.6 %collective-permute-start.71 = (bf16[100,3200]{1,0:T(8,128)(2,1)}, bf16[100,3200]{1,0:T(8,128)(2,1)}, u32[]{:S(2)}, u32[]{:S(2)}) collective-permute-start(bf16[100,3200]{1,0:T(8,128)(2,1)} %get-tuple-element.384), channel_id=1, source_target_pairs={{0,4},{1,5},{2,6},{3,7},{4,0},{5,1},{6,2},{7,3},{8,12},{9,13},{10,... | collective-permute-start | bytes 1920008 | tf_op jit(solution)/shard_map/ppermute | solution.py:24
  1279.0 58.6 %collective-permute-start.72 = (bf16[100,3200]{1,0:T(8,128)(2,1)}, bf16[100,3200]{1,0:T(8,128)(2,1)}, u32[]{:S(2)}, u32[]{:S(2)}) collective-permute-start(bf16[100,3200]{1,0:T(8,128)(2,1)} %get-tuple-element.385), channel_id=1, source_target_pairs={{0,12},{1,13},{2,14},{3,15},{4,8},{5,9},{6,10},{7,11},{8,4},{9,5},... | collective-permute-start | bytes 1920008 | tf_op jit(solution)/shard_map/ppermute | solution.py:24
  (287 other events, 3731.1 us)
Sparse Core Ops, SparseCore 0:
  264.3 158.7 all-gather.2
  434.8 156.8 all-gather.4
  665.4 101.8 reduce-scatter.18
  770.2 70.9 reduce-scatter.20
  844.2 85.0 reduce-scatter.22
  932.2 46.9 reduce-scatter.24
  982.5 74.7 reduce-scatter.26
  1060.6 87.1 reduce-scatter.28

commit v3 on v2

--- a/solution.py
+++ b/solution.py
@@ -224,19 +224,21 @@
 
 
 def sum_first(left, right):
-    return chip_swap(left[3], 2), chip_swap(right[3], 1), chip_swap(left[2], 2), chip_swap(right[1], 1)
+    return chip_swap(left[3], 2), chip_swap(right[3], 1)
 
 
 def sum_second(left, right, got):
-    to_x = (left[1].astype(F32) + got[0].astype(F32)).astype(BF)
-    to_y = (right[2].astype(F32) + got[1].astype(F32)).astype(BF)
+    to_x = jnp.stack([(left[1].astype(F32) + got[0].astype(F32)).astype(BF), right[1]])
+    to_y = jnp.stack([left[2], (right[2].astype(F32) + got[1].astype(F32)).astype(BF)])
     return chip_swap(to_x, 1), chip_swap(to_y, 2)
 
 
-def sum_whole(left, right, got, last):
-    left = left[0].astype(F32) + got[2].astype(F32) + last[0].astype(F32)
-    right = right[0].astype(F32) + got[3].astype(F32) + last[1].astype(F32)
-    return left.astype(BF), right.astype(BF)
+def sum_whole(left, right, last):
+    from_x, from_y = last
+    return [
+        (own.astype(F32) + from_x[i].astype(F32) + from_y[i].astype(F32)).astype(BF)
+        for i, own in enumerate((left[0], right[0]))
+    ]
 
 
 def bits_of(count):
@@ -526,17 +528,15 @@
     mlp_shards = two(w_fc[0], w_proj[0])
     m0, m0_yours = by_side(mlp_shards[0])
     m1, m1_yours = by_side(mlp_shards[1])
-    vector_rows = vectors[None]
-    for bit in range(bits):
-        vector_rows = gather_bit(vector_rows, bit)
-    a0_line, a1, m0, m0_yours, m1, m1_yours, vector_rows = fence(
-        a0_line, a1, m0, m0_yours, m1, m1_yours, vector_rows
-    )
+    a0_line, a1, m0, m0_yours, m1, m1_yours, vectors = fence(a0_line, a1, m0, m0_yours, m1, m1_yours, vectors)
 
     a0_quarter = line_rows(*a0_line)
     a0_got = plane_first(a0_quarter)
     a1_line = line_first(a1, a1)
     m0_near = chip_swap(m0_yours, 4)
+    vector_rows = vectors[None]
+    for bit in range(bits):
+        vector_rows = gather_bit(vector_rows, bit)
     own_inputs = lax.dynamic_index_in_dim(inputs, core, 0, False)
     own_cotangent = lax.dynamic_index_in_dim(cotangent, core, 0, False)
     order_line = (place[:, None] == natural_line[None, :]).astype(BF)
@@ -652,10 +652,11 @@
     normed_both, context_both, qkv_both, attn_both = attn_factors(
         second_normed, second_context, qkv_mine, qkv_yours, attn_mine, attn_yours
     )
-    q1_terms = owner_terms(line_by_owner(normed_both), qkv_both)
-    o1_terms = owner_terms(line_by_owner(context_both), attn_both)
-    first_up_all, q1_terms, o1_terms, f1_sum = fence(first_up_all, q1_terms, o1_terms, f1_sum)
-    q1_sum, o1_sum = plane_sum(q1_terms), plane_sum(o1_terms)
+    a1_terms = owner_terms(
+        line_by_owner(jnp.concatenate([normed_both, context_both], axis=0)), beside(qkv_both, attn_both)
+    )
+    first_up_all, a1_terms, f1_sum = fence(first_up_all, a1_terms, f1_sum)
+    a1_sum = plane_sum(a1_terms)
     first_pre_grad, part = mlp_back(first_up_all, first_pre, *mlp_first)
     first_pre_grad, part = fence(first_pre_grad, part)
     grad_norm = reduce_tokens(part)
@@ -663,13 +664,11 @@
     p0_terms = owner_terms(side_by_owner(first_up_all), first_act)
     grad_norm, f0_terms, p0_terms, p1_sum = fence(grad_norm, f0_terms, p0_terms, p1_sum)
     f0_sum, p0_sum = plane_sum(f0_terms), plane_sum(p0_terms)
-    m1_pieces = line_pieces((f1_sum, p1_sum), False)
-    m1_got = line_sum_first(m1_pieces)
     first_mid_grad, first_da, attn_mine, attn_yours, heads_grad, first_gain_two, first_bias_two = attn_out_back(
         first_up, grad_norm, first_norm_two, *attn_first
     )
-    heads_grad, first_mid_grad, m1_got, attn_mine, attn_yours, q1_sum = fence(
-        heads_grad, first_mid_grad, m1_got, attn_mine, attn_yours, q1_sum
+    heads_grad, first_mid_grad, attn_mine, attn_yours, f1_sum, p1_sum = fence(
+        heads_grad, first_mid_grad, attn_mine, attn_yours, f1_sum, p1_sum
     )
     def by_section(first, second):
         own = jnp.where(core == 0, first, second)
@@ -688,9 +687,11 @@
         second_packed,
         second_pre_grad,
     )
-    back, o1_sum, section_outputs, second_vectors = fence(back, o1_sum, section_outputs, second_vectors)
-    a1_pieces = line_pieces((q1_sum, o1_sum), True)
-    a1_got = line_sum_first(a1_pieces)
+    back, section_outputs, second_vectors, f1_sum, p1_sum = fence(
+        back, section_outputs, second_vectors, f1_sum, p1_sum
+    )
+    m1_pieces = line_pieces((f1_sum, p1_sum), False)
+    m1_got = line_sum_first(m1_pieces)
     first_grad, first_packed, qkv_mine, qkv_yours, first_gain_one, first_bias_one = attn_qkv_back(
         back, first_mid_grad, first_norm_one, *attn_first
     )
@@ -702,8 +703,10 @@
     a0_right = line_terms(
         jnp.concatenate([normed_both, context_both], axis=0), beside(qkv_both[:, width:], attn_both)
     )
-    a0_left, a0_right, first_grad_low = fence(a0_left, a0_right, first_grad_low)
+    a0_left, a0_right, first_grad_low, m1_got, a1_sum = fence(a0_left, a0_right, first_grad_low, m1_got, a1_sum)
     a0_got = sum_first(a0_left, a0_right)
+    a1_pieces = line_pieces((a1_sum,), True)
+    a1_got = line_sum_first(a1_pieces)
     a0_got, a1_got, f0_sum, p0_sum, first_grad_low, first_packed = fence(
         a0_got, a1_got, f0_sum, p0_sum, first_grad_low, first_packed
     )
@@ -728,7 +731,7 @@
     )
     a0_last, m0_got, input_grads, vector_rows = fence(a0_last, m0_got, input_grads, vector_rows)
     vector_own = reduce_vector(vector_rows)
-    a0_pieces = line_pieces(sum_whole(a0_left, a0_right, a0_got, a0_last), True)
+    a0_pieces = line_pieces(sum_whole(a0_left, a0_right, a0_last), True)
     a0_got = line_sum_first(a0_pieces)
 
     def matrix_grads(attn_pieces, attn_got, mlp_pieces, mlp_got):

time: 1380 us -> 1350 us (0.978)
  starting transfers between devices: 150 us -> 121 us
  waiting for transfers between devices: 508 us -> 531 us
  local copies, waits for them, and re-layouts: 177 us -> 160 us
    all_to_all x7, waiting for transfers between devices: 76.3 us -> 106 us  [pack_exchange(): return lax.all_to_all(value, 'fsdp', 0, 0, axis_index_groups=groups)]
    ppermute x50 -> x48, starting transfers between devices: 113 us -> 86.2 us  [chip_swap(): return lax.ppermute(value, 'fsdp', [(i, i ^ mask) for i in range(count)])]
    ppermute x50 -> x48, waiting for transfers between devices: 392 us -> 379 us  [chip_swap(): return lax.ppermute(value, 'fsdp', [(i, i ^ mask) for i in range(count)])]
    unnamed x14 -> x12, waiting for transfers between devices: 32.6 us -> 36.6 us
    unnamed x491 -> x454, local copies, waits for them, and re-layouts: 47.8 us -> 51 us
    dot_general x14 -> x13, matrix products: 44.6 us -> 46.9 us  [dot_rows(): lax.dot_general(left, right, (((0,), (0,)), ((), ())), preferred_element_...]
  transfers between devices with their start and end apart: 92 -> 89, of which waited for: 43 -> 45; matrix products, arithmetic and copies ran while one was open for 38% -> 38% of each run, Pallas kernels for 4% -> 4%
where the time goes in v3:
time: 1350 us; the launch traced here: 1330 us
  waiting for transfers between devices  531 us (39%)
  matrix products  314 us (23%)
  local copies, waits for them, and re-layouts  160 us (12%)
  other arithmetic  124 us (9%)
  starting transfers between devices  121 us (9%)
  Pallas kernels  49.1 us (4%)
  between operations  18.6 us (1%)
  blocking collectives  16.4 us (1%)
    ppermute x48, waiting for transfers between devices, chip_swap(): return lax.ppermute(value, 'fsdp', [(i, i ^ mask) for i in range(count)])  379 us
    dot_general x34, matrix products, dot(): return jnp.dot(left, right, preferred_element_type=F32)  140 us
    all_to_all x7, waiting for transfers between devices, pack_exchange(): return lax.all_to_all(value, 'fsdp', 0, 0, axis_index_groups=groups)  106 us
    dot_general x23, matrix products, dot_cols(): lax.dot_general(left, right, (((1,), (1,)), ((), ())), preferred_element_...  102 us
    ppermute x48, starting transfers between devices, chip_swap(): return lax.ppermute(value, 'fsdp', [(i, i ^ mask) for i in range(count)])  86.2 us
    unnamed x454, local copies, waits for them, and re-layouts  51 us
    dot_general x13, matrix products, dot_rows(): lax.dot_general(left, right, (((0,), (0,)), ((), ())), preferred_element_...  46.9 us
    unnamed x12, waiting for transfers between devices  36.6 us
  transfers between devices with their start and end apart: 89, of which 45 were waited for; matrix products, arithmetic and copies ran while one was open for 38% of the time, Pallas kernels for 4%

profile of v3, /device:TPU:0, one launch (start us, length us, event | category | flops | bytes accessed | tf_op | source)
XLA Modules:
  0.0 1334.2 jit_solution(282495968290304740)
XLA Ops:
  42.1 15.0 %collective-permute-done.2 = bf16[2,100,1600]{2,0,1:T(2,128)(2,1)S(1)} collective-permute-done((bf16[2,100,1600]{2,0,1:T(2,128)(2,1)S(1)}, bf16[2,100,1600]{2,0,1:T(2,128)(2,1)S(1)}, u32[]{:S(2)}, u32[]{:S(2)}) %collective-permute-start.2) | collective-permute-done | bytes 640032 | tf_op jit(solution)/shard_map/ppermute | solution.py:24
  57.0 26.5 %collective-permute-done.1 = bf16[2,100,1600]{2,0,1:T(2,128)(2,1)S(1)} collective-permute-done((bf16[2,100,1600]{2,0,1:T(2,128)(2,1)S(1)}, bf16[2,100,1600]{2,0,1:T(2,128)(2,1)S(1)}, u32[]{:S(2)}, u32[]{:S(2)}) %collective-permute-start.1) | collective-permute-done | bytes 640032 | tf_op jit(solution)/shard_map/ppermute | solution.py:24
  129.3 18.4 %collective-permute-done.7 = bf16[2,100,1600]{2,0,1:T(2,128)(2,1)} collective-permute-done((bf16[2,100,1600]{2,0,1:T(2,128)(2,1)}, bf16[2,100,1600]{2,0,1:T(2,128)(2,1)}, u32[]{:S(2)}, u32[]{:S(2)}) %collective-permute-start.7) | collective-permute-done | bytes 640032 | tf_op jit(solution)/shard_map/ppermute | solution.py:24
  185.3 12.4 collective-permute-done.15
  214.5 36.8 %collective-permute-done.21 = bf16[2,400,1600]{2,1,0:T(8,128)(2,1)} collective-permute-done((bf16[2,400,1600]{2,1,0:T(8,128)(2,1)}, bf16[2,400,1600]{2,1,0:T(8,128)(2,1)}, u32[]{:S(2)}, u32[]{:S(2)}) %collective-permute-start.21) | collective-permute-done | bytes 2560032 | tf_op jit(solution)/shard_map/ppermute | solution.py:24
  296.0 21.4 %collective-permute-done.27 = bf16[400,1600]{1,0:T(8,128)(2,1)S(1)} collective-permute-done((bf16[400,1600]{1,0:T(8,128)(2,1)S(1)}, bf16[400,1600]{1,0:T(8,128)(2,1)S(1)}, u32[]{:S(2)}, u32[]{:S(2)}) %collective-permute-start.27) | collective-permute-done | bytes 1280032 | tf_op jit(solution)/shard_map/ppermute | solution.py:24
  322.4 27.6 %all-to-all-done.q_ref.k_ref.v_ref = bf16[8,768,128]{2,1,0:T(8,128)(2,1)S(1)} async-done(((bf16[8,768,128]{2,1,0:T(8,128)(2,1)}), bf16[8,768,128]{2,1,0:T(8,128)(2,1)S(1)}, u32[]{:S(2)}, u32[]{:S(2)}) %all-to-all-start) | async-done | bytes 1572896 | tf_op jit(solution)/shard_map/all_to_all | solution.py:211
  350.1 12.4 shard_map.254
  397.2 27.8 %collective-permute-done.29 = bf16[2,100,1600]{2,1,0:T(8,128)(2,1)} collective-permute-done((bf16[2,100,1600]{2,1,0:T(8,128)(2,1)}, bf16[2,100,1600]{2,1,0:T(8,128)(2,1)}, u32[]{:S(2)}, u32[]{:S(2)}) %collective-permute-start.29) | collective-permute-done | bytes 640032 | tf_op jit(solution)/shard_map/ppermute | solution.py:24
  432.5 11.6 pad_maximum_fusion.5
  446.6 11.9 pad_maximum_fusion.4
  481.9 23.7 %collective-permute-done.33 = bf16[128,1600]{0,1:T(8,128)(2,1)S(1)} collective-permute-done((bf16[128,1600]{0,1:T(8,128)(2,1)S(1)}, bf16[128,1600]{0,1:T(8,128)(2,1)S(1)}, u32[]{:S(2)}, u32[]{:S(2)}) %collective-permute-start.33) | collective-permute-done | bytes 409632 | tf_op jit(solution)/shard_map/ppermute | solution.py:24
  537.6 53.9 %all-to-all-done.2.q_ref.k_ref.v_ref = bf16[8,768,128]{2,1,0:T(8,128)(2,1)} async-done(((bf16[8,768,128]{2,1,0:T(8,128)(2,1)}), bf16[8,768,128]{2,1,0:T(8,128)(2,1)}, u32[]{:S(2)}, u32[]{:S(2)}) %all-to-all-start.2) | async-done | bytes 1572896 | tf_op jit(solution)/shard_map/all_to_all | solution.py:211
  591.5 13.4 %shard_map.255 = (bf16[8,256,128]{2,1,0:T(8,128)(2,1)}, bf16[4,1024,1024]{2,1,0:T(8,128)(2,1)}) custom-call(bf16[8,768,128]{2,1,0:T(8,128)(2,1)} %all-to-all-done.2.q_ref.k_ref.v_ref, bf16[8,768,128]{2,1,0:T(8,128)(2,1)} %all-to-all-done.2.q_ref.k_ref.v_ref, bf16[8,768,128]{2,1,0:T(8,128)(2,1)} %all-to-all-done.2.q_ref.k_ref.v_ref, s32[1,1024]{1,0:T(1,128)S(1)} %bitcast.398, ...), custom_call_target="tpu_custom_call" | custom-call | flops 12000000000 | bytes 12000000 | tf_op jit(solution)/shard_map/pallas_call | solution.py:146
  704.6 16.4 %all_to_all.40.d_ref = bf16[8,256,128]{2,1,0:T(8,128)(2,1)S(1)} all-to-all(bf16[8,256,128]{2,1,0:T(8,128)(2,1)S(1)} %fusion.147), channel_id=1, replica_groups={{0,1,2,3,4,5,6,7},{8,9,10,11,12,13,14,15},{16,17,18,19,20,21,22,23},{24..., dimensions={0} | all-to-all | bytes 1048576 | tf_op jit(solution)/shard_map/all_to_all | solution.py:211
  721.0 11.7 shard_map.256
  745.2 21.0 %all-to-all-done.5 = bf16[8,768,128]{2,1,0:T(8,128)(2,1)} async-done(((bf16[8,768,128]{2,1,0:T(8,128)(2,1)}), bf16[8,768,128]{2,1,0:T(8,128)(2,1)}, u32[]{:S(2)}, u32[]{:S(2)}) %all-to-all-start.5) | async-done | bytes 1572896 | tf_op jit(solution)/shard_map/all_to_all | solution.py:211
  1035.9 25.7 %collective-permute-done.49 = bf16[100,3200]{1,0:T(8,128)(2,1)} collective-permute-done((bf16[100,3200]{1,0:T(8,128)(2,1)S(1)}, bf16[100,3200]{1,0:T(8,128)(2,1)}, u32[]{:S(2)}, u32[]{:S(2)}) %collective-permute-start.49) | collective-permute-done | bytes 640032 | tf_op jit(solution)/shard_map/ppermute | solution.py:24
  1071.6 27.2 %collective-permute-start.55 = (bf16[100,3200]{1,0:T(8,128)(2,1)}, bf16[100,3200]{1,0:T(8,128)(2,1)}, u32[]{:S(2)}, u32[]{:S(2)}) collective-permute-start(bf16[100,3200]{1,0:T(8,128)(2,1)} %get-tuple-element.351), channel_id=1, source_target_pairs={{0,4},{1,5},{2,6},{3,7},{4,0},{5,1},{6,2},{7,3},{8,12},{9,13},{10,... | collective-permute-start | bytes 1920008 | tf_op jit(solution)/shard_map/ppermute | solution.py:24
  1104.0 35.9 %reduce-scatter.24.cloned.1.call-done = bf16[1,400,1600]{2,1,0:T(8,128)(2,1)} async-done(((bf16[4,400,1600]{2,1,0:T(8,128)(2,1)}), bf16[1,400,1600]{2,1,0:T(8,128)(2,1)}) %reduce-scatter.24.cloned.1.call-update) | async-done | bytes 1280016
  1178.5 25.6 %collective-permute-done.59 = bf16[100,3200]{1,0:T(8,128)(2,1)} collective-permute-done((bf16[100,3200]{1,0:T(8,128)(2,1)}, bf16[100,3200]{1,0:T(8,128)(2,1)}, u32[]{:S(2)}, u32[]{:S(2)}) %collective-permute-start.59) | collective-permute-done | bytes 640032 | tf_op jit(solution)/shard_map/ppermute | solution.py:24
  1204.2 14.0 %collective-permute-done.60 = bf16[100,3200]{1,0:T(8,128)(2,1)S(1)} collective-permute-done((bf16[100,3200]{1,0:T(8,128)(2,1)S(1)}, bf16[100,3200]{1,0:T(8,128)(2,1)S(1)}, u32[]{:S(2)}, u32[]{:S(2)}) %collective-permute-start.60) | collective-permute-done | bytes 640032 | tf_op jit(solution)/shard_map/ppermute | solution.py:24
  1261.4 25.4 %collective-permute-done.67 = f32[1,1,1200]{2,1,0:T(1,128)S(1)} collective-permute-done((f32[1,1,1200]{2,1,0:T(1,128)S(1)}, f32[1,1,1200]{2,1,0:T(1,128)S(1)}, u32[]{:S(2)}, u32[]{:S(2)}) %collective-permute-start.67) | collective-permute-done | bytes 4832 | tf_op jit(solution)/shard_map/ppermute | solution.py:24
  1290.2 15.3 %collective-permute-done.70 = bf16[100,3200]{1,0:T(8,128)(2,1)S(1)} collective-permute-done((bf16[100,3200]{1,0:T(8,128)(2,1)S(1)}, bf16[100,3200]{1,0:T(8,128)(2,1)S(1)}, u32[]{:S(2)}, u32[]{:S(2)}) %collective-permute-start.70) | collective-permute-done | bytes 640032 | tf_op jit(solution)/shard_map/ppermute | solution.py:24
  (1027 shorter events, 784.3 us)
Async XLA Ops:
  7.2 417.8 %all-gather.3.cloned.1.call-start = ((), (), s32[]{:S(2)}) async-start(), calls=%async_computation.13 | async-start | bytes 11520000 | tf_op jit(solution)/shard_map/all_gather | solution.py:330
  98.1 58.7 %collective-permute-start.6 = (bf16[2,400,1600]{2,1,0:T(8,128)(2,1)}, bf16[2,400,1600]{2,1,0:T(8,128)(2,1)}, u32[]{:S(2)}, u32[]{:S(2)}) collective-permute-start(bf16[2,400,1600]{2,1,0:T(8,128)(2,1)} %reshape.869), channel_id=1, source_target_pairs={{0,2},{1,3},{2,0},{3,1},{4,6},{5,7},{6,4},{7,5},{8,10},{9,11},{10,... | collective-permute-start | bytes 7680008 | tf_op jit(solution)/shard_map/ppermute | solution.py:24
  98.6 58.4 %collective-permute-start.5 = (bf16[2,400,1600]{2,1,0:T(8,128)(2,1)}, bf16[2,400,1600]{2,1,0:T(8,128)(2,1)}, u32[]{:S(2)}, u32[]{:S(2)}) collective-permute-start(bf16[2,400,1600]{2,1,0:T(8,128)(2,1)} %reshape.869), channel_id=1, source_target_pairs={{0,1},{1,0},{2,3},{3,2},{4,5},{5,4},{6,7},{7,6},{8,9},{9,8},{10,11... | collective-permute-start | bytes 7680008 | tf_op jit(solution)/shard_map/ppermute | solution.py:24
  183.2 68.1 %collective-permute-start.21 = (bf16[2,400,1600]{2,1,0:T(8,128)(2,1)}, bf16[2,400,1600]{2,1,0:T(8,128)(2,1)}, u32[]{:S(2)}, u32[]{:S(2)}) collective-permute-start(bf16[2,400,1600]{2,1,0:T(8,128)(2,1)} %reshape.870), channel_id=1, source_target_pairs={{0,2},{1,3},{2,0},{3,1},{4,6},{5,7},{6,4},{7,5},{8,10},{9,11},{10,... | collective-permute-start | bytes 7680008 | tf_op jit(solution)/shard_map/ppermute | solution.py:24
  183.8 72.1 %collective-permute-start.20 = (bf16[2,400,1600]{2,1,0:T(8,128)(2,1)}, bf16[2,400,1600]{2,1,0:T(8,128)(2,1)}, u32[]{:S(2)}, u32[]{:S(2)}) collective-permute-start(bf16[2,400,1600]{2,1,0:T(8,128)(2,1)} %reshape.870), channel_id=1, source_target_pairs={{0,1},{1,0},{2,3},{3,2},{4,5},{5,4},{6,7},{7,6},{8,9},{9,8},{10,11... | collective-permute-start | bytes 7680008 | tf_op jit(solution)/shard_map/ppermute | solution.py:24
  185.3 70.6 %collective-permute-start.18 = (bf16[2,400,1600]{2,1,0:T(8,128)(2,1)}, bf16[2,400,1600]{2,1,0:T(8,128)(2,1)}, u32[]{:S(2)}, u32[]{:S(2)}) collective-permute-start(bf16[2,400,1600]{2,1,0:T(8,128)(2,1)} %collective-permute-done.5), channel_id=1, source_target_pairs={{0,16},{16,0},{1,17},{17,1},{2,18},{18,2},{3,19},{19,3},{4,20},{20... | collective-permute-start | bytes 7680008 | tf_op jit(solution)/shard_map/ppermute | solution.py:28
  197.7 58.2 %collective-permute-start.19 = (bf16[2,400,1600]{2,1,0:T(8,128)(2,1)}, bf16[2,400,1600]{2,1,0:T(8,128)(2,1)}, u32[]{:S(2)}, u32[]{:S(2)}) collective-permute-start(bf16[2,400,1600]{2,1,0:T(8,128)(2,1)} %collective-permute-done.6), channel_id=1, source_target_pairs={{0,16},{16,0},{1,17},{17,1},{2,18},{18,2},{3,19},{19,3},{4,20},{20... | collective-permute-start | bytes 7680008 | tf_op jit(solution)/shard_map/ppermute | solution.py:28
  366.2 250.3 %all-gather.5.cloned.1.call-start = ((), (), s32[]{:S(2)}) async-start(), calls=%async_computation.14 | async-start | bytes 11520000 | tf_op jit(solution)/shard_map/all_gather | solution.py:330
  444.1 64.7 %collective-permute-start.35 = (bf16[1600,1600]{1,0:T(8,128)(2,1)}, bf16[1600,1600]{1,0:T(8,128)(2,1)}, u32[]{:S(2)}, u32[]{:S(2)}) collective-permute-start(bf16[1600,1600]{1,0:T(8,128)(2,1)} %pad_maximum_fusion.5), channel_id=1, source_target_pairs={{0,16},{16,0},{1,17},{17,1},{2,18},{18,2},{3,19},{19,3},{4,20},{20... | collective-permute-start | bytes 15360008 | tf_op jit(solution)/shard_map/ppermute | solution.py:28
  532.6 58.8 %all-to-all-start.2 = ((bf16[8,768,128]{2,1,0:T(8,128)(2,1)}), bf16[8,768,128]{2,1,0:T(8,128)(2,1)}, u32[]{:S(2)}, u32[]{:S(2)}) async-start(bf16[8,768,128]{2,1,0:T(8,128)(2,1)} %pad_dynamic-update-slice_fusion), calls=%async_computation.2 | async-start | bytes 3145728 | tf_op jit(solution)/shard_map/all_to_all | solution.py:211
  608.5 215.2 %reduce-scatter.16.cloned.1.call-start = ((), (), s32[]{:S(2)}) async-start(), calls=%async_computation.15 | async-start | bytes 6656000
  738.2 153.2 %reduce-scatter.18.cloned.1.call-start = ((), (), s32[]{:S(2)}) async-start(), calls=%async_computation.16 | async-start | bytes 6656000
  738.8 323.9 %reduce-scatter.20.cloned.1.call-start = ((), (), s32[]{:S(2)}) async-start(), calls=%async_computation.17 | async-start | bytes 12800000
  823.8 280.2 %reduce-scatter.22.cloned.1.call-start = ((), (), s32[]{:S(2)}) async-start(), calls=%async_computation.18 | async-start | bytes 6656000
  860.1 65.0 %collective-permute-start.47 = (bf16[128,1600]{0,1:T(8,128)(2,1)}, bf16[128,1600]{0,1:T(8,128)(2,1)}, u32[]{:S(2)}, u32[]{:S(2)}) collective-permute-start(bf16[128,1600]{0,1:T(8,128)(2,1)} %get-tuple-element.450), channel_id=1, source_target_pairs={{0,16},{16,0},{1,17},{17,1},{2,18},{18,2},{3,19},{19,3},{4,20},{20... | collective-permute-start | bytes 1228808 | tf_op jit(solution)/shard_map/ppermute | solution.py:28
  955.9 184.0 %reduce-scatter.24.cloned.1.call-start = ((), (), s32[]{:S(2)}) async-start(), calls=%async_computation.19 | async-start | bytes 6656000
  1062.7 79.0 %collective-permute-start.52 = (bf16[400,1600]{1,0:T(8,128)(2,1)}, bf16[400,1600]{1,0:T(8,128)(2,1)}, u32[]{:S(2)}, u32[]{:S(2)}) collective-permute-start(bf16[400,1600]{1,0:T(8,128)(2,1)} %convolution_convert_fusion.9), channel_id=1, source_target_pairs={{0,2},{1,3},{2,0},{3,1},{4,6},{5,7},{6,4},{7,5},{8,10},{9,11},{10,... | collective-permute-start | bytes 3840008 | tf_op jit(solution)/shard_map/ppermute | solution.py:24
  1063.8 78.0 %collective-permute-start.53 = (bf16[400,1600]{1,0:T(8,128)(2,1)}, bf16[400,1600]{1,0:T(8,128)(2,1)}, u32[]{:S(2)}, u32[]{:S(2)}) collective-permute-start(bf16[400,1600]{1,0:T(8,128)(2,1)} %convolution_convert_fusion.5), channel_id=1, source_target_pairs={{0,1},{1,0},{2,3},{3,2},{4,5},{5,4},{6,7},{7,6},{8,9},{9,8},{10,11... | collective-permute-start | bytes 3840008 | tf_op jit(solution)/shard_map/ppermute | solution.py:24
  1068.3 71.6 %collective-permute-start.56 = (bf16[100,3200]{1,0:T(8,128)(2,1)}, bf16[100,3200]{1,0:T(8,128)(2,1)}, u32[]{:S(2)}, u32[]{:S(2)}) collective-permute-start(bf16[100,3200]{1,0:T(8,128)(2,1)} %get-tuple-element.350), channel_id=1, source_target_pairs={{0,12},{1,13},{2,14},{3,15},{4,8},{5,9},{6,10},{7,11},{8,4},{9,5},... | collective-permute-start | bytes 1920008 | tf_op jit(solution)/shard_map/ppermute | solution.py:24
  1071.6 68.3 %collective-permute-start.55 = (bf16[100,3200]{1,0:T(8,128)(2,1)}, bf16[100,3200]{1,0:T(8,128)(2,1)}, u32[]{:S(2)}, u32[]{:S(2)}) collective-permute-start(bf16[100,3200]{1,0:T(8,128)(2,1)} %get-tuple-element.351), channel_id=1, source_target_pairs={{0,4},{1,5},{2,6},{3,7},{4,0},{5,1},{6,2},{7,3},{8,12},{9,13},{10,... | collective-permute-start | bytes 1920008 | tf_op jit(solution)/shard_map/ppermute | solution.py:24
  1162.6 60.5 %collective-permute-start.58 = (bf16[2,400,1600]{2,1,0:T(8,128)(2,1)}, bf16[2,400,1600]{2,1,0:T(8,128)(2,1)}, u32[]{:S(2)}, u32[]{:S(2)}) collective-permute-start(bf16[2,400,1600]{2,1,0:T(8,128)(2,1)} %pad_maximum_fusion.7), channel_id=1, source_target_pairs={{0,2},{1,3},{2,0},{3,1},{4,6},{5,7},{6,4},{7,5},{8,10},{9,11},{10,... | collective-permute-start | bytes 7680008 | tf_op jit(solution)/shard_map/ppermute | solution.py:24
  1167.4 60.2 %collective-permute-start.57 = (bf16[2,400,1600]{2,1,0:T(8,128)(2,1)}, bf16[2,400,1600]{2,1,0:T(8,128)(2,1)}, u32[]{:S(2)}, u32[]{:S(2)}) collective-permute-start(bf16[2,400,1600]{2,1,0:T(8,128)(2,1)} %pad_maximum_fusion.6), channel_id=1, source_target_pairs={{0,1},{1,0},{2,3},{3,2},{4,5},{5,4},{6,7},{7,6},{8,9},{9,8},{10,11... | collective-permute-start | bytes 7680008 | tf_op jit(solution)/shard_map/ppermute | solution.py:24
  1245.0 71.1 %collective-permute-start.74 = (f32[100,3200]{1,0:T(8,128)}, f32[100,3200]{1,0:T(8,128)}, u32[]{:S(2)}, u32[]{:S(2)}) collective-permute-start(f32[100,3200]{1,0:T(8,128)} %get-tuple-element.343), channel_id=1, source_target_pairs={{0,16},{16,0},{1,17},{17,1},{2,18},{18,2},{3,19},{19,3},{4,20},{20... | collective-permute-start | bytes 3840008 | tf_op jit(solution)/shard_map/ppermute | solution.py:28
  1247.4 62.3 %collective-permute-start.73 = (f32[100,3200]{1,0:T(8,128)}, f32[100,3200]{1,0:T(8,128)}, u32[]{:S(2)}, u32[]{:S(2)}) collective-permute-start(f32[100,3200]{1,0:T(8,128)} %get-tuple-element.345), channel_id=1, source_target_pairs={{0,16},{16,0},{1,17},{17,1},{2,18},{18,2},{3,19},{19,3},{4,20},{20... | collective-permute-start | bytes 3840008 | tf_op jit(solution)/shard_map/ppermute | solution.py:28
  (265 other events, 3303.1 us)
Sparse Core Ops, SparseCore 0:
  259.3 157.3 all-gather.2
  429.0 156.7 all-gather.4
  682.3 86.4 reduce-scatter.15
  771.6 64.0 reduce-scatter.17
  838.7 139.7 reduce-scatter.19
  981.3 67.5 reduce-scatter.21
  1052.0 87.9 reduce-scatter.23
